TPU v7x, 256 devices: a whole 4x4x8 slice. The times are simulated.
256 devices in a mesh: pairs: 32 (over y, x, core), ri: 8 (over z).
Axes of the slice: x: 4, y: 4, z: 8, core: 2. Of those that a mesh axis runs over, the one named last changes fastest.
Arguments:
- atom_blocks: bfloat16 [512, 20, 14336], P('pairs', None, 'ri'), may hold values from -6 to 6
- domains: int32 [1024, 12], P('pairs'), may hold values from 0 to 511, as said below
- pno_counts: int32 [1024], P('pairs'), may hold values from 20 to 200
- pno_coeffs: bfloat16 [1024, 240, 256], P('pairs'), may hold values from -0.375 to 0.375
- amplitudes: bfloat16 [1024, 256, 256], P(('pairs', 'ri')), may hold values from -3 to 3
- pno_energies: float32 [1024, 256], P(('pairs', 'ri')), may hold values from 0.2 to 4
Outputs:
- residual: float32 [1024, 256, 256], P(('pairs', 'ri'))
Inputs may be any that keep to these rules, and one draw needn't show every extreme that they name: `domains`: atom a belongs to owner a // 16 along pairs. The pairs of one device (aligned blocks of 32 rows) name atoms of at most 16 owners and at most 3 distinct atoms of any one owner; in every draw some owner gives exactly 3 distinct atoms to every device.
All inputs are finite; a program needn't handle non-finite values.
Results may differ from a plain program's by a relative error of at most 0.0003.
Values may be sent and summed in bfloat16 or wider, within the bound.
A program may use at most 192 MiB of HBM per device.

v0:
```python
import jax
import jax.numpy as jnp
from jax import lax
from jax.sharding import PartitionSpec as P

NAUX = 14336
CAP = 3


def on_device(atom_blocks, domains, pno_counts, pno_coeffs, amplitudes, pno_energies):
    owners = lax.axis_size("pairs")
    lane_count = lax.axis_size("ri")
    atom_dev, band, aux_cols = atom_blocks.shape
    pair_dev, domain_size = domains.shape
    slot_count = pno_coeffs.shape[2]
    flat_ids = domains.reshape(-1)
    atom_ids = jnp.arange(owners * atom_dev, dtype=jnp.int32)
    matches = flat_ids[:, None] == atom_ids[None, :]
    needed = jnp.any(matches, axis=0).reshape(owners, atom_dev)
    position = jnp.cumsum(needed.astype(jnp.int32), axis=1) - 1
    slot_base = jnp.arange(owners, dtype=jnp.int32)[:, None] * CAP + position
    slot_place = jnp.sum(jnp.where(matches, slot_base.reshape(-1)[None, :], 0), axis=1)
    slot_rows = slot_place.reshape(pair_dev, domain_size)
    chosen = needed[:, :, None] & (
        position[:, :, None] == jnp.arange(CAP, dtype=jnp.int32)[None, None, :]
    )
    local_plus = jnp.arange(1, atom_dev + 1, dtype=jnp.int32)[None, :, None]
    requests = jnp.sum(jnp.where(chosen, local_plus, 0), axis=1)
    wanted = lax.all_to_all(requests, "pairs", split_axis=0, concat_axis=0, tiled=True)
    picked = jnp.take(atom_blocks, jnp.maximum(wanted - 1, 0), axis=0)
    picked = jnp.where((wanted > 0)[:, :, None, None], picked, jnp.zeros_like(picked))
    arrived = lax.all_to_all(picked, "pairs", split_axis=0, concat_axis=0, tiled=True)
    received = arrived.reshape(owners * CAP, band, aux_cols)
    contract = (((0,), (0,)), ((), ()))

    def project(coeff, block, count):
        raw = lax.dot_general(coeff, block, contract, preferred_element_type=jnp.float32)
        valid = jnp.arange(slot_count, dtype=jnp.int32) < count
        return jnp.where(valid[:, None], raw, jnp.zeros_like(raw)).astype(jnp.bfloat16)

    def vectors_of(item):
        block = jnp.take(received, item[1], axis=0).reshape(domain_size * band, aux_cols)
        return project(item[0], block, item[2])

    def partial_products(item):
        vectors = vectors_of(item)
        return jnp.dot(vectors, vectors.T, preferred_element_type=jnp.float32)

    terms = lax.map(partial_products, (pno_coeffs, slot_rows, pno_counts))
    products = lax.psum_scatter(terms, "ri", scatter_dimension=0, tiled=True) / NAUX
    sub_count = pair_dev // lane_count
    start = lax.axis_index("ri") * sub_count
    counts_here = lax.dynamic_slice_in_dim(pno_counts, start, sub_count, 0)
    valid_here = jnp.arange(slot_count, dtype=jnp.int32)[None, :] < counts_here[:, None]
    amp_full = amplitudes.astype(jnp.float32)
    coupled = jnp.einsum("pac,pbc->pab", products, amp_full, precision=lax.Precision.HIGHEST)
    energy_sum = pno_energies[:, :, None] + pno_energies[:, None, :]
    result = products + coupled + energy_sum * amp_full
    mask = valid_here[:, :, None] & valid_here[:, None, :]
    return jnp.where(mask, result, jnp.zeros_like(result))


def solution(mesh):
    placed = (
        P("pairs", None, "ri"),
        P("pairs", None),
        P("pairs"),
        P("pairs", None, None),
        P(("pairs", "ri"), None, None),
        P(("pairs", "ri"), None),
    )
    return jax.shard_map(
        on_device,
        mesh=mesh,
        in_specs=placed,
        out_specs=P(("pairs", "ri"), None, None),
        check_vma=False,
    )
```

profile of v0, /device:TPU:1, one launch (start us, length us, event | category | flops | bytes accessed | tf_op | source)
XLA Modules:
  0.0 562.2 jit_solution(6205887838191745155)
XLA Ops:
  8.4 15.3 %all_to_all.14 = s32[32,1,3]{2,1,0:T(1,128)S(1)} all-to-all(s32[32,1,3]{2,1,0:T(1,128)S(1)} %copy.45), channel_id=1, replica_groups=mesh['pairs'=32,'ri'=8] {'pairs'}, dimensions={0} | all-to-all | bytes 768 | tf_op jit(solution)/shard_map/all_to_all | solution.py:29
  24.3 28.8 %gather_fusion.1 = bf16[96,20,1792]{2,0,1:T(8,128)(2,1)} fusion(bf16[16,20,1792]{2,0,1:T(8,128)(2,1)S(1)} %copy-done, s32[1024]{0:T(1024)S(1)} %pad_clamp_fusion.1), kind=kCustom, calls=%fused_computation.1 | custom fusion | bytes 13762944 | tf_op jit(solution)/shard_map/jit(_take)/gather | solution.py:30
  53.0 10.0 %copy.51 = bf16[96,20,1792]{2,1,0:T(8,128)(2,1)} copy(bf16[96,20,1792]{2,0,1:T(8,128)(2,1)} %gather_fusion.1) | data formatting | bytes 13762560 | tf_op jit(solution)/shard_map/jit(_take)/gather | solution.py:30
  63.0 7.6 %select_select_fusion = bf16[32,3,20,1792]{3,2,1,0:T(8,128)(2,1)} fusion(bf16[32,3,20,1792]{3,2,1,0:T(8,128)(2,1)} %bitcast.38, pred[32,3]{1,0:T(8,128)(4,1)S(1)} %bitcast.40, pred[32,3]{1,0:T(8,128)(4,1)S(1)} %bitcast.39), kind=kLoop, calls=%fused_computation.21 | loop fusion | flops 6881280 | bytes 13762752 | tf_op jit(solution)/shard_map/jit(_where)/select_n | solution.py:31
  70.6 5.9 %all-to-all-start.1 = ((bf16[32,3,20,1792]{3,2,1,0:T(8,128)(2,1)}), bf16[32,3,20,1792]{3,2,1,0:T(8,128)(2,1)}, u32[]{:S(2)}, u32[]{:S(2)}) async-start(bf16[32,3,20,1792]{3,2,1,0:T(8,128)(2,1)} %select_select_fusion), calls=%async_computation.1 | async-start | bytes 16515072 | tf_op jit(solution)/shard_map/all_to_all | solution.py:32
  77.0 97.7 %all-to-all-done.1 = bf16[32,3,20,1792]{3,2,1,0:T(8,128)(2,1)} async-done(((bf16[32,3,20,1792]{3,2,1,0:T(8,128)(2,1)}), bf16[32,3,20,1792]{3,2,1,0:T(8,128)(2,1)}, u32[]{:S(2)}, u32[]{:S(2)}) %all-to-all-start.1) | async-done | bytes 6881312 | tf_op jit(solution)/shard_map/all_to_all | solution.py:32
  174.7 278.4 %while.10 = (s32[]{:T(128)}, f32[32,256,256]{2,1,0:T(8,128)}, s32[32]{0:T(128)S(1)}, bf16[32,240,256]{2,1,0:T(8,128)(2,1)}, s32[32,12]{1,0:T(8,128)S(1)}, /*index=5*/bf16[96,20,1792]{2,1,0:T(8,128)(2,1)}, s32[]{:T(128)}) while((s32[]{:T(128)}, f32[32,256,256]{2,1,0:T(8,128)}, s32[32]{0:T(128)S(1)}, bf16[32,240,256]{2,1,0:T(8,128)(2,1)}, ...), condition=%wide.region_5.6_spmd, body=%wide.region_4.5_spmd.sunk | while | flops 456430944 | bytes 6412141 | solution.py:49
  174.7 4.0 gather_fusion
  183.4 4.0 gather_fusion
  192.1 4.0 gather_fusion
  197.8 3.0 fusion.30
  200.8 4.0 gather_fusion
  206.5 3.0 fusion.30
  209.5 4.0 gather_fusion
  215.2 3.0 fusion.30
  218.2 4.0 gather_fusion
  223.9 3.0 fusion.30
  226.9 4.0 gather_fusion
  232.6 3.0 fusion.30
  235.6 4.0 gather_fusion
  241.3 3.0 fusion.30
  244.3 4.0 gather_fusion
  250.0 3.0 fusion.30
  253.0 4.0 gather_fusion
  261.7 4.0 gather_fusion
  270.4 4.0 gather_fusion
  276.1 3.0 fusion.30
  279.1 4.0 gather_fusion
  284.8 3.0 fusion.30
  287.8 4.0 gather_fusion
  293.5 3.0 fusion.30
  296.5 4.0 gather_fusion
  305.2 4.0 gather_fusion
  310.9 3.0 fusion.30
  313.9 4.0 gather_fusion
  322.6 4.0 gather_fusion
  331.3 4.0 gather_fusion
  337.0 3.0 fusion.30
  340.0 4.0 gather_fusion
  345.7 3.0 fusion.30
  348.7 4.0 gather_fusion
  354.4 3.0 fusion.30
  357.4 4.0 gather_fusion
  363.1 3.0 fusion.30
  366.1 4.0 gather_fusion
  371.8 3.0 fusion.30
  374.8 4.0 gather_fusion
  380.5 3.0 fusion.30
  383.5 4.0 gather_fusion
  389.2 3.0 fusion.30
  392.2 4.0 gather_fusion
  397.9 3.0 fusion.30
  400.9 4.0 gather_fusion
  406.6 3.0 fusion.30
  409.6 4.0 gather_fusion
  415.3 3.0 fusion.30
  418.3 4.0 gather_fusion
  424.0 3.0 fusion.30
  427.0 4.0 gather_fusion
  435.7 4.0 gather_fusion
  444.4 4.0 gather_fusion
  450.0 3.0 fusion.30
  453.2 98.9 %reduce-scatter.2.cloned.1.call-done = f32[4,256,256]{2,1,0:T(8,128)} async-done(((f32[32,256,256]{2,1,0:T(8,128)}), f32[4,256,256]{2,1,0:T(8,128)}) %reduce-scatter.2.cloned.1.call-update) | async-done | bytes 1048592 | tf_op jit(solution)/shard_map/reduce_scatter | solution.py:50
  552.1 3.2 fusion.15
  (270 shorter events, 84.5 us)
Async XLA Ops:
  6.5 17.7 %copy-start = (bf16[16,20,1792]{2,0,1:T(8,128)(2,1)S(1)}, bf16[16,20,1792]{2,0,1:T(8,128)(2,1)}, u32[]{:S(2)}) copy-start(bf16[16,20,1792]{2,0,1:T(8,128)(2,1)} %param.8) | copy-start | bytes 3440644
  70.6 104.1 %copy-start.3 = (s32[32]{0:T(128)S(1)}, s32[32]{0:T(128)}, u32[]{:S(2)}) copy-start(s32[32]{0:T(128)} %param.10) | copy-start | bytes 388
  70.6 104.1 %all-to-all-start.1 = ((bf16[32,3,20,1792]{3,2,1,0:T(8,128)(2,1)}), bf16[32,3,20,1792]{3,2,1,0:T(8,128)(2,1)}, u32[]{:S(2)}, u32[]{:S(2)}) async-start(bf16[32,3,20,1792]{3,2,1,0:T(8,128)(2,1)} %select_select_fusion), calls=%async_computation.1 | async-start | bytes 16515072 | tf_op jit(solution)/shard_map/all_to_all | solution.py:32
  76.5 475.6 %reduce-scatter.2.cloned.1.call-start = ((), (), s32[]{:S(2)}) async-start(), calls=%async_computation.3 | async-start | bytes 9437184 | tf_op jit(solution)/shard_map/reduce_scatter | solution.py:50
  453.1 99.1 %copy-start.1 = (bf16[4,256,256]{2,1,0:T(8,128)(2,1)S(1)}, bf16[4,256,256]{2,1,0:T(8,128)(2,1)}, u32[]{:S(2)}) copy-start(bf16[4,256,256]{2,1,0:T(8,128)(2,1)} %param.12) | copy-start | bytes 1572868
  453.1 99.1 %copy-start.2 = (f32[4,256]{1,0:T(4,128)S(1)}, f32[4,256]{1,0:T(4,128)}, u32[]{:S(2)}) copy-start(f32[4,256]{1,0:T(4,128)} %param.13) | copy-start | bytes 12292
Sparse Core Ops, SparseCore 0:
  453.2 98.8 reduce-scatter.1
where the time goes:
time: 565 us; the launch traced here: 562 us
  waiting for transfers between devices  197 us (35%)
  local copies, waits for them, and re-layouts  194 us (34%)
  matrix products  99.1 us (18%)
  other arithmetic  36.3 us (6%)
  blocking collectives  15.3 us (3%)
  between operations  13.5 us (2%)
  starting transfers between devices  5.97 us (1%)
    gather x32, local copies, waits for them, and re-layouts, vectors_of(): jnp.take(received, item[1], axis=0).reshape(domain_size * band, aux_cols)  127 us
    reduce_scatter x1, waiting for transfers between devices, on_device(): lax.psum_scatter(terms, 'ri', scatter_dimension=0, tiled=True) / NAUX  98.9 us
    all_to_all x1, waiting for transfers between devices, on_device(): lax.all_to_all(picked, 'pairs', split_axis=0, concat_axis=0, tiled=True)  97.7 us
    dot_general x32, matrix products, partial_products(): return jnp.dot(vectors, vectors.T, preferred_element_type=jnp.float32)  96 us
    gather x2, local copies, waits for them, and re-layouts, on_device(): picked = jnp.take(atom_blocks, jnp.maximum(wanted - 1, 0), axis=0)  38.8 us
    lt x32, other arithmetic, project(): valid = jnp.arange(slot_count, dtype=jnp.int32) < count  21.7 us
    dynamic_slice x32, local copies, waits for them, and re-layouts, on_device(): terms = lax.map(partial_products, (pno_coeffs, slot_rows, pno_counts))  21.1 us
    all_to_all x1, blocking collectives, on_device(): lax.all_to_all(requests, 'pairs', split_axis=0, concat_axis=0, tiled=True)  15.3 us
  transfers between devices with their start and end apart: 2, of which 2 were waited for; matrix products, arithmetic and copies ran while one was open for 0% of the time, Pallas kernels for 0%

commit v1 on v0

v1 whole, which is shorter than its diff:
```python
import jax
import jax.numpy as jnp
from jax import lax
from jax.experimental import pallas as pl
from jax.experimental.pallas import tpu as pltpu
from jax.sharding import PartitionSpec as P

NAUX = 14336
CAP = 3
MAXPNO = 200
MAIN = 16
REM = 4
SPLIT = 128
REST = MAXPNO - SPLIT
LANES = 128
MIB = 1 << 20
RING = 4
CORES = 2
ATOMS = 16
DOM = 12
BAND = MAIN + REM
PICKS = RING * CAP
HALF = PICKS // 2
DEPTH = 256
DUO = SPLIT + 3 * REST + 8
TILES = (4, 4, 3, 3)
FIRST = (0, 4, 8, 11)
MESH = pl.DeviceIdType.MESH


def params(mib, **kw):
    return pltpu.CompilerParams(vmem_limit_bytes=mib * MIB, **kw)


def widths(chunk):
    return TILES[chunk] * LANES, TILES[chunk] * LANES + LANES


class Ports:
    def __init__(self, chunk, gather_to, deliver_to, wire, ring, send, relay, recv, out_sems, in_sems, core):
        self.gather_to, self.deliver_to, self.core = gather_to, deliver_to, core
        self.wire, self.ring, self.send, self.relay, self.recv = wire, ring, send, relay, recv
        self.out_sems, self.in_sems, self.chunk = out_sems, in_sems, chunk

    def copy(self, src, dst, out_at, in_at, to):
        return pltpu.make_async_remote_copy(
            src_ref=src,
            dst_ref=dst,
            send_sem=self.out_sems.at[self.chunk, out_at],
            recv_sem=self.in_sems.at[self.chunk, in_at],
            device_id={"pairs": to},
            device_id_type=MESH,
        )

    def gather_first(self):
        up = self.copy(self.wire, self.ring.at[2], 0, 1, self.gather_to(1, self.core))
        down = self.copy(self.wire, self.ring.at[0], 1, 0, self.gather_to(3, self.core))
        return up, down

    def gather_second(self):
        half = ATOMS // 2
        low, high = pl.ds(0, half), pl.ds(half, half)
        up = self.copy(self.ring.at[2, low], self.ring.at[1, low], 2, 2, self.gather_to(1, self.core))
        down = self.copy(self.ring.at[0, high], self.ring.at[1, high], 3, 3, self.gather_to(3, self.core))
        return up, down

    def place(self, rel, core):
        return (rel * CORES + core) * PICKS

    def far(self):
        up = self.copy(self.send.at[2, :, pl.ds(0, HALF)], self.relay.at[0], 4, 4, self.deliver_to(1, self.core))
        down = self.copy(self.send.at[2, :, pl.ds(HALF, HALF)], self.relay.at[1], 5, 5, self.deliver_to(3, self.core))
        return up, down

    def near(self):
        copies = []
        for n, step in enumerate((1, 3)):
            for core in range(CORES):
                dst = self.recv.at[pl.ds(self.place(RING - step, self.core), PICKS)]
                at = 6 + 2 * n
                copies.append(self.copy(self.send.at[step, core], dst, at + core, at + self.core, self.deliver_to(step, core)))
        other = 1 - self.core
        dst = self.recv.at[pl.ds(self.place(0, self.core), PICKS)]
        copies.append(self.copy(self.send.at[0, other], dst, 10, 10, self.deliver_to(0, other)))
        return copies

    def own(self):
        return pltpu.make_async_copy(
            self.send.at[0, self.core],
            self.recv.at[pl.ds(self.place(0, self.core), PICKS)],
            self.in_sems.at[self.chunk, 11],
        )

    def onward(self):
        copies = []
        for way, step in enumerate((1, 3)):
            for core in range(CORES):
                dst = self.recv.at[pl.ds(self.place(2, self.core) + way * HALF, HALF)]
                at = 12 + 2 * way
                copies.append(self.copy(self.relay.at[way, core], dst, at + core, at + self.core, self.deliver_to(step, core)))
        return copies

    def start_gather(self):
        for copy in self.gather_first():
            copy.start()

    def forward_gather(self):
        up, down = self.gather_second()
        first_up, first_down = self.gather_first()
        first_up.wait_recv()
        up.start()
        first_down.wait_recv()
        down.start()

    def finish_gather(self):
        for copy in self.gather_second():
            copy.wait_recv()

    def start_delivery(self):
        for copy in self.far() + tuple(self.near()):
            copy.start()
        self.own().start()

    def forward_delivery(self):
        far, onward = self.far(), self.onward()
        for way in range(2):
            far[way].wait_recv()
            for copy in onward[2 * way : 2 * way + 2]:
                copy.start()

    def finish_delivery(self):
        for n, step in enumerate((1, 3)):
            for core in range(CORES):
                dst = self.recv.at[pl.ds(self.place(step, core), PICKS)]
                at = 6 + 2 * (1 - n)
                self.copy(dst, dst, at + core, at + core, self.deliver_to(1, self.core)).wait_recv()
        other = 1 - self.core
        dst = self.recv.at[pl.ds(self.place(0, other), PICKS)]
        self.copy(dst, dst, 10, 10, self.deliver_to(1, self.core)).wait_recv()
        self.own().wait()
        for way in range(2):
            for core in range(CORES):
                dst = self.recv.at[pl.ds(self.place(2, core) + way * HALF, HALF)]
                at = 12 + 2 * way
                self.copy(dst, dst, at + core, at + core, self.deliver_to(1, self.core)).wait_recv()

    def finish_served(self):
        for copy in self.far() + tuple(self.near()):
            copy.wait_send()

    def finish_sends(self):
        for copy in self.gather_first() + self.gather_second() + tuple(self.onward()):
            copy.wait_send()


def main_kernel(
    blocks, domains, coeff_hbm, out, *scratch
):
    wires, rings, sends, relays, recvs = (scratch[4 * n : 4 * n + 4] for n in range(5))
    asked, asked_smem, tables, places, request, ids, perm_main, perm_rest = scratch[20:28]
    coeff, coeff_t, perm, blk, total, sums, fresh = scratch[28:35]
    out_sems, in_sems, ask_out, ask_in, local_sems, sum_out, sum_in = scratch[35:42]
    me = lax.axis_index("pairs")
    at_z = lax.axis_index("ri")
    planes = 2 * (sums.shape[1] - 1)
    above, below = lax.rem(at_z + 1, planes), lax.rem(at_z + planes - 1, planes)
    core = lax.rem(me, CORES)
    chip = lax.div(me, CORES)
    at_x = lax.rem(chip, RING)
    at_y = lax.div(chip, RING)

    def along_x(step, to_core):
        return (at_y * RING + lax.rem(at_x + step, RING)) * CORES + to_core

    def along_y(step, to_core):
        return (lax.rem(at_y + step, RING) * RING + at_x) * CORES + to_core

    peers = []
    for to_core in range(2):
        for step in range(1, RING):
            peers.append((along_y(step, to_core), step * CORES + to_core, (RING - step) * CORES + core))
            peers.append(
                (along_x(step, to_core), (RING + step) * CORES + to_core, (2 * RING - step) * CORES + core)
            )
    peers.append((along_x(0, 1 - core), 1 - core, core))

    fetch = pltpu.make_async_copy(coeff_hbm, coeff, local_sems.at[0])
    fetch.start()
    barrier = pltpu.get_barrier_semaphore()
    for peer, _, _ in peers:
        pl.semaphore_signal(barrier, inc=1, device_id={"pairs": peer}, device_id_type=MESH)
    for plane in (above, below):
        pl.semaphore_signal(barrier, inc=1, device_id={"ri": plane}, device_id_type=MESH)

    def ask(n):
        peer, _, there = peers[n]
        return pltpu.make_async_remote_copy(
            src_ref=request,
            dst_ref=asked.at[there],
            send_sem=ask_out.at[n],
            recv_sem=ask_in.at[there],
            device_id={"pairs": peer},
            device_id_type=MESH,
        )

    ports = []
    for chunk in range(4):
        gather_to, deliver_to = (along_x, along_y) if chunk % 2 == 0 else (along_y, along_x)
        ports.append(
            Ports(
                chunk, gather_to, deliver_to, wires[chunk], rings[chunk], sends[chunk],
                relays[chunk], recvs[chunk], out_sems, in_sems, core,
            )
        )

    square = (ATOMS * MAIN, ATOMS * MAIN)
    out_at = lax.broadcasted_iota(jnp.int32, square, 0)
    from_at = lax.broadcasted_iota(jnp.int32, square, 1)
    band_at, atom_at = out_at % MAIN, out_at // MAIN
    perm_main[...] = jnp.where(band_at * ATOMS + atom_at == from_at, 1.0, 0.0).astype(jnp.bfloat16)
    rest_at = (band_at // REM) * (REM * ATOMS) + (band_at % REM) * ATOMS + atom_at
    perm_rest[...] = jnp.where(rest_at == from_at, 1.0, 0.0).astype(jnp.bfloat16)

    def form(chunk):
        cols, _ = widths(chunk)
        begin = FIRST[chunk] * LANES
        flat = blocks[:MAIN, :, begin : begin + cols].reshape(MAIN * ATOMS, cols)
        main = jnp.dot(perm_main[...], flat, preferred_element_type=jnp.float32).astype(jnp.bfloat16)
        wires[chunk][:, :, :cols] = main.reshape(ATOMS, MAIN, cols)
        rest = blocks[MAIN:, :, begin : begin + cols].reshape(REM * ATOMS, cols)
        stacked = jnp.concatenate([rest[:, q * LANES : (q + 1) * LANES] for q in range(TILES[chunk])], axis=0)
        depth = stacked.shape[0]
        late = jnp.dot(perm_rest[:, :depth], stacked, preferred_element_type=jnp.float32).astype(jnp.bfloat16)
        wires[chunk][:, :, cols:] = late.reshape(ATOMS, MAIN, LANES)

    form(0)
    form(1)

    ids[...] = jnp.zeros_like(ids)
    pairs = domains.shape[1]
    fold = LANES // pairs
    ids[: domains.shape[0], :pairs] = domains[...]
    held = ids[...]
    lane = lax.broadcasted_iota(jnp.int32, held.shape, 1)
    turned = [held if n == 0 else pltpu.roll(held, n * pairs, 1) for n in range(fold)]
    lines = []
    for line in range(DOM // fold):
        row = jnp.zeros((1, LANES), jnp.int32)
        for n in range(fold):
            k = line * fold + n
            row = jnp.where(lane[:1] // pairs == n, turned[n][k : k + 1], row)
        lines.append(row)
    flat_shape = (ATOMS * RING * RING * CORES, LANES)
    atom = lax.broadcasted_iota(jnp.int32, flat_shape, 0)
    lane_at = lax.broadcasted_iota(jnp.int32, flat_shape, 1)
    named = jnp.zeros(flat_shape, jnp.int32)
    for line in lines:
        named = jnp.where(atom == line, 1, named)
    named = jnp.broadcast_to(jnp.max(named, axis=1, keepdims=True), flat_shape)
    local = atom % ATOMS
    owner = atom // ATOMS
    rank = named
    for shift in (1, 2, 4, 8):
        rank = rank + jnp.where(local >= shift, pltpu.roll(rank, shift, 0), 0)
    own_lane = jnp.where((owner == lane_at) & (named > 0), local, 0)
    for j in range(CAP):
        request[j : j + 1, :] = jnp.sum(jnp.where(rank == j + 1, own_lane, 0), axis=0, keepdims=True)
    request[CAP:, :] = jnp.zeros((8 - CAP, LANES), jnp.int32)

    pl.semaphore_wait(barrier, len(peers) + 2)
    ports[0].start_gather()
    ports[1].start_gather()
    for n in range(len(peers)):
        ask(n).start()
    own_ask = pltpu.make_async_copy(request, asked.at[core], local_sems.at[1])
    own_ask.start()

    form(2)
    form(3)
    owner_chip = owner // CORES
    rel_x = (owner_chip + RING - at_x) % RING
    rel_y = (owner_chip // RING + RING - at_y) % RING
    owner_core = owner % CORES
    place_x = ((rel_y * CORES + owner_core) * RING + rel_x) * CAP + rank - 1
    place_y = ((rel_x * CORES + owner_core) * RING + rel_y) * CAP + rank - 1
    tables[...] = jnp.zeros_like(tables)
    for n, line in enumerate(lines):
        for table, place in enumerate((place_x, place_y)):
            tables[table, n : n + 1, :] = jnp.sum(jnp.where(atom == line, place, 0), axis=0, keepdims=True)
    table_copy = pltpu.make_async_copy(tables, places, local_sems.at[3])
    table_copy.start()
    table_copy.wait()

    shape = (DEPTH, DOM * BAND)
    row = lax.broadcasted_iota(jnp.int32, shape, 0)
    col = lax.broadcasted_iota(jnp.int32, shape, 1)
    split = DOM * MAIN
    late = row - split
    source = jnp.where(
        row < split,
        (row // MAIN) * BAND + row % MAIN,
        (late // REM) * BAND + MAIN + late % REM,
    )
    perm[...] = jnp.where((source == col) & (row < DOM * BAND), 1.0, 0.0).astype(jnp.bfloat16)
    for n in range(2):
        blk[n, DOM * BAND :, :] = jnp.zeros((DEPTH - DOM * BAND, blk.shape[2]), jnp.bfloat16)
    fetch.wait()

    def prepare(begin, end):
        def turn(pair, _):
            ordered = jnp.dot(perm[...], coeff[pair], preferred_element_type=jnp.float32)
            coeff_t[pair] = ordered.T[:MAXPNO].astype(jnp.bfloat16)
            return 0

        lax.fori_loop(begin, end, turn, 0)

    half_pairs = coeff.shape[0] // 2
    quarter = half_pairs // 2
    prepare(0, half_pairs - REM)
    ports[0].forward_gather()
    ports[1].forward_gather()
    ports[2].start_gather()
    ports[3].start_gather()
    prepare(half_pairs - REM, half_pairs + REM)

    own_ask.wait()
    for n in range(len(peers)):
        _, here, _ = peers[n]
        pltpu.make_async_remote_copy(
            src_ref=request,
            dst_ref=asked.at[here],
            send_sem=ask_out.at[n],
            recv_sem=ask_in.at[here],
            device_id={"pairs": peers[n][0]},
            device_id_type=MESH,
        ).wait_recv()
    to_smem = pltpu.make_async_copy(asked, asked_smem, local_sems.at[2])
    to_smem.start()
    to_smem.wait()

    def pick(chunk):
        port = ports[chunk]
        owner_of = along_x if chunk % 2 == 0 else along_y

        def serve(dest, _):
            line = dest if chunk % 2 == 0 else jnp.where(dest < CORES, dest, dest + RING * CORES)
            step, to_core = dest // CORES, dest % CORES
            for r in range(RING):
                for j in range(CAP):
                    atom = asked_smem[line, j, owner_of(r, core)]
                    found = port.wire[atom] if r == 0 else port.ring[r - 1, atom]
                    port.send[step, to_core, r * CAP + j] = found
            return 0

        lax.fori_loop(0, RING * CORES, serve, 0)

    for chunk in (0, 1):
        ports[chunk].finish_gather()
        pick(chunk)
        ports[chunk].start_delivery()
    for chunk in (2, 3):
        ports[chunk].forward_gather()
    prepare(half_pairs + REM, half_pairs + quarter)
    ports[0].forward_delivery()
    ports[1].forward_delivery()
    for chunk in (2, 3):
        ports[chunk].finish_gather()
        pick(chunk)
    prepare(half_pairs + quarter, 2 * half_pairs)
    for chunk in (2, 3):
        ports[chunk - 2].finish_served()
        ports[chunk].start_delivery()

    pack_row = lax.broadcasted_iota(jnp.int32, (SPLIT, LANES), 0)
    pack_col = lax.broadcasted_iota(jnp.int32, (SPLIT, LANES), 1)
    rest_row = lax.broadcasted_iota(jnp.int32, (REST, REST), 0)
    rest_col = lax.broadcasted_iota(jnp.int32, (REST, REST), 1)

    def assemble(pair, slot, chunks):
        base = MAIN * DOM
        begin = 0
        for table, chunk in enumerate(chunks):
            cols, _ = widths(chunk)
            upper = lax.broadcasted_iota(jnp.int32, (8, LANES), 0) < REM
            at = [places[table, k // fold, (k % fold) * pairs + pair] for k in range(DOM)]
            for k in range(DOM):
                blk[slot, MAIN * k : MAIN * (k + 1), begin : begin + cols] = recvs[chunk][at[k], :, :cols]
            for k in range(0, DOM, 4):
                rest = [recvs[chunk][at[k + n], :, cols:].astype(jnp.float32) for n in range(4)]
                for half in range((TILES[chunk] + 1) // 2):
                    parts = [r[8 * half : 8 * half + 8] for r in rest]
                    shifted = [pltpu.roll(part, REM, 0) for part in parts]
                    for q in range(2 * half, min(2 * half + 2, TILES[chunk])):
                        first, second = (parts, shifted) if q % 2 == 0 else (shifted, parts)
                        low = jnp.where(upper, first[0], second[1])
                        high = jnp.where(upper, first[2], second[3])
                        both = jnp.concatenate([low, high], axis=0).astype(jnp.bfloat16)
                        tile = slice(begin + q * LANES, begin + (q + 1) * LANES)
                        blk[slot, base + REM * k : base + REM * (k + 4), tile] = both
            begin += cols
        return begin

    def multiply(pair, slot, cols):
        weights = coeff_t[pair]
        result = jnp.zeros((MAXPNO, MAXPNO), jnp.float32)
        for at in range(0, cols, 256):
            vec = jnp.dot(weights, blk[slot, :, at : at + 256], preferred_element_type=jnp.float32)
            vec = vec.astype(jnp.bfloat16)
            result += lax.dot_general(vec, vec, (((1,), (1,)), ((), ())), preferred_element_type=jnp.float32)
        return result

    def first_half(step, _):
        for n in range(2):
            cols = assemble(2 * step + n, n, (0, 1))
        for n in range(2):
            total[2 * step + n] = multiply(2 * step + n, n, cols)
        return 0

    group = coeff.shape[0] // planes
    half_ring = planes // 2
    part = DUO // 2

    def chain(way, step, duo, piece):
        rows = pl.ds(piece * part, part)
        return pltpu.make_async_remote_copy(
            src_ref=sums.at[way, step, duo, rows],
            dst_ref=sums.at[way, step + 1, duo, rows],
            send_sem=sum_out.at[(way * half_ring + step) * 2 + duo, piece],
            recv_sem=sum_in.at[(way * half_ring + step) * 2 + duo, piece],
            device_id={"ri": jnp.where(way == 0, above, below)},
            device_id_type=MESH,
        )

    def second_half(owner, duo):
        first = owner * group + 2 * duo
        for n in range(2):
            cols = assemble(first + n, n, (2, 3))
        whole = [total[first + n] + multiply(first + n, n, cols) for n in range(2)]
        here, there = [w[:SPLIT, :SPLIT] for w in whole]
        fresh[:SPLIT, :] = jnp.where(pack_row >= pack_col, here, there)
        for n in range(2):
            fresh[SPLIT + n * REST : SPLIT + (n + 1) * REST, :] = whole[n][SPLIT:, :SPLIT]
        at = SPLIT + 2 * REST
        low_here, low_there = [w[SPLIT:, SPLIT:] for w in whole]
        fresh[at : at + REST, :REST] = jnp.where(rest_row >= rest_col, low_here, low_there)
        at += REST
        fresh[at : at + 1, :] = jnp.sum(jnp.where(pack_row == pack_col, there, 0.0), axis=0, keepdims=True)
        fresh[at + 1 : at + 2, :REST] = jnp.sum(
            jnp.where(rest_row == rest_col, low_there, 0.0), axis=0, keepdims=True
        )

    def send_on(item, _):
        later = jnp.maximum(item - 2, 0)
        turn = later % 4
        opening = item < 2
        step = jnp.where(opening, 0, 1 + later // 4)
        way = jnp.where(opening, item, turn % 2)
        early = jnp.logical_and(jnp.logical_not(opening), turn < 2)
        duo = jnp.where(early, 1 - way, way)
        away = jnp.where(way == 0, half_ring - step, half_ring + step)
        second_half(lax.rem(at_z + away, planes), duo)
        alone = jnp.logical_or(opening, jnp.logical_and(early, step == 1))

        @pl.when(alone)
        def _():
            sums[way, step, duo] = fresh[...]
            for piece in range(2):
                chain(way, step, duo, piece).start()

        @pl.when(jnp.logical_not(alone))
        def _():
            for piece in range(2):
                rows = slice(piece * part, (piece + 1) * part)
                chain(way, step - 1, duo, piece).wait_recv()
                sums[way, step, duo, rows, :] = sums[way, step, duo, rows, :] + fresh[rows, :]
                chain(way, step, duo, piece).start()

        return 0

    def send_done(item, _):
        later = jnp.maximum(item - 2, 0)
        turn = later % 4
        opening = item < 2
        step = jnp.where(opening, 0, 1 + later // 4)
        way = jnp.where(opening, item, turn % 2)
        early = jnp.logical_and(jnp.logical_not(opening), turn < 2)
        duo = jnp.where(early, 1 - way, way)
        for piece in range(2):
            chain(way, step, duo, piece).wait_send()
        return 0

    ports[0].finish_delivery()
    ports[1].finish_delivery()
    lax.fori_loop(0, half_pairs // 2, first_half, 0)
    ports[2].forward_delivery()
    ports[3].forward_delivery()
    lax.fori_loop(half_pairs // 2, half_pairs, first_half, 0)
    ports[2].finish_delivery()
    ports[3].finish_delivery()
    fresh[...] = jnp.zeros_like(fresh)
    items = 2 + 4 * (half_ring - 1)
    lax.fori_loop(0, items, send_on, 0)
    for duo in range(2):
        second_half(at_z, duo)
        for piece in range(2):
            rows = slice(piece * part, (piece + 1) * part)
            for way in range(2):
                chain(way, half_ring - 1, duo, piece).wait_recv()
            arrived = sums[0, half_ring, duo, rows, :] + sums[1, half_ring, duo, rows, :]
            out[duo, rows, :] = arrived + fresh[rows, :]
    lax.fori_loop(0, items, send_done, 0)
    for chunk in (2, 3):
        ports[chunk].finish_served()
    for n in range(len(peers)):
        ask(n).wait_send()
    for chunk in range(4):
        ports[chunk].finish_sends()


def pair_products(blocks, domains, coeff, planes):
    pair_dev, depth, slots = coeff.shape
    lines = 2 * RING * CORES
    wide = [widths(chunk)[1] for chunk in range(4)]
    half_cols = widths(0)[0] + widths(1)[0]
    bf16 = jnp.bfloat16
    scratch = [pltpu.VMEM((ATOMS, MAIN, w), bf16) for w in wide]
    scratch += [pltpu.VMEM((RING - 1, ATOMS, MAIN, w), bf16) for w in wide]
    scratch += [pltpu.VMEM((RING, CORES, PICKS, MAIN, w), bf16) for w in wide]
    scratch += [pltpu.VMEM((2, CORES, HALF, MAIN, w), bf16) for w in wide]
    scratch += [pltpu.VMEM((RING * CORES * PICKS, MAIN, w), bf16) for w in wide]
    scratch += [
        pltpu.VMEM((lines, 8, LANES), jnp.int32),
        pltpu.SMEM((lines, 8, LANES), jnp.int32),
        pltpu.VMEM((2, 8, LANES), jnp.int32),
        pltpu.SMEM((2, 8, LANES), jnp.int32),
        pltpu.VMEM((8, LANES), jnp.int32),
        pltpu.VMEM((16, LANES), jnp.int32),
        pltpu.VMEM((ATOMS * MAIN, ATOMS * MAIN), bf16),
        pltpu.VMEM((ATOMS * MAIN, ATOMS * MAIN), bf16),
        pltpu.VMEM((pair_dev, depth, slots), bf16),
        pltpu.VMEM((pair_dev, MAXPNO, DEPTH), bf16),
        pltpu.VMEM((DEPTH, depth), bf16),
        pltpu.VMEM((2, DEPTH, half_cols), bf16),
        pltpu.VMEM((pair_dev, MAXPNO, MAXPNO), jnp.float32),
        pltpu.VMEM((2, planes // 2 + 1, 2, DUO, LANES), jnp.float32),
        pltpu.VMEM((DUO, LANES), jnp.float32),
        pltpu.SemaphoreType.DMA((4, 16)),
        pltpu.SemaphoreType.DMA((4, 16)),
        pltpu.SemaphoreType.DMA((lines,)),
        pltpu.SemaphoreType.DMA((lines,)),
        pltpu.SemaphoreType.DMA((4,)),
        pltpu.SemaphoreType.DMA((2 * planes, 2)),
        pltpu.SemaphoreType.DMA((2 * planes, 2)),
    ]
    return pl.pallas_call(
        main_kernel,
        out_shape=jax.ShapeDtypeStruct((2, DUO, LANES), jnp.float32),
        in_specs=[
            pl.BlockSpec(memory_space=pltpu.VMEM),
            pl.BlockSpec(memory_space=pltpu.VMEM),
            pl.BlockSpec(memory_space=pl.ANY),
        ],
        out_specs=pl.BlockSpec(memory_space=pltpu.VMEM),
        scratch_shapes=scratch,
        compiler_params=params(60, collective_id=0, has_side_effects=True),
    )(blocks, domains, coeff)


def tail_kernel(counts, packed, amp, energy_row, energy_col, out, wide):
    slots = amp.shape[1]
    step = pl.program_id(0)
    row = lax.broadcasted_iota(jnp.int32, (SPLIT, LANES), 0)
    col = lax.broadcasted_iota(jnp.int32, (SPLIT, LANES), 1)
    low_row, low_col = row[:REST], col[:REST]
    full_row = lax.broadcasted_iota(jnp.int32, (slots, slots), 0)
    full_col = lax.broadcasted_iota(jnp.int32, (slots, slots), 1)
    for n in range(2):
        first = packed[0, :SPLIT, :]
        rest = packed[0, SPLIT + 2 * REST : SPLIT + 3 * REST, :]
        if n == 0:
            first = jnp.where(row >= col, first, 0.0)
            rest = jnp.where(low_row >= low_col, rest, 0.0)
        else:
            at = SPLIT + 3 * REST
            first = jnp.where(row < col, first, jnp.where(row == col, packed[0, at : at + 1, :], 0.0))
            rest = jnp.where((low_row < low_col) & (low_col < REST), rest, 0.0)
            rest = jnp.where(low_row == low_col, packed[0, at + 1 : at + 2, :], rest)
        wide[n, :SPLIT, :LANES] = first
        wide[n, :SPLIT, LANES:] = jnp.zeros((SPLIT, slots - LANES), jnp.float32)
        wide[n, SPLIT : SPLIT + REST, :LANES] = packed[0, SPLIT + n * REST : SPLIT + (n + 1) * REST, :]
        wide[n, SPLIT : SPLIT + REST, LANES:] = rest
        wide[n, MAXPNO:, :] = jnp.zeros((slots - MAXPNO, slots), jnp.float32)
    for n in range(2):
        count = counts[2 * step + n]
        held = wide[n]
        products = held + jnp.where(full_row == full_col, 0.0, held.T)
        valid = (full_row < count) & (full_col < count)
        products = jnp.where(valid, products / NAUX, 0.0)
        amps = amp[n]
        contract = (((1,), (1,)), ((), ()))
        high = products.astype(jnp.bfloat16)
        left = products - high.astype(jnp.float32)
        mid = left.astype(jnp.bfloat16)
        low = (left - mid.astype(jnp.float32)).astype(jnp.bfloat16)
        coupled = lax.dot_general(low, amps, contract, preferred_element_type=jnp.float32)
        coupled += lax.dot_general(mid, amps, contract, preferred_element_type=jnp.float32)
        coupled += lax.dot_general(high, amps, contract, preferred_element_type=jnp.float32)
        energies = energy_col[n] + energy_row[n]
        result = products + coupled + energies * amps.astype(jnp.float32)
        out[n] = jnp.where(valid, result, 0.0)


def tail(counts, packed, amp, energy):
    subs, slots, _ = amp.shape
    return pl.pallas_call(
        tail_kernel,
        out_shape=jax.ShapeDtypeStruct((subs, slots, slots), jnp.float32),
        grid=(subs // 2,),
        in_specs=[
            pl.BlockSpec(memory_space=pltpu.SMEM),
            pl.BlockSpec((1, DUO, LANES), lambda i: (i, 0, 0)),
            pl.BlockSpec((2, slots, slots), lambda i: (i, 0, 0)),
            pl.BlockSpec((2, 1, slots), lambda i: (i, 0, 0)),
            pl.BlockSpec((2, slots, 1), lambda i: (i, 0, 0)),
        ],
        out_specs=pl.BlockSpec((2, slots, slots), lambda i: (i, 0, 0)),
        scratch_shapes=[pltpu.VMEM((2, slots, slots), jnp.float32)],
        compiler_params=params(32),
    )(counts, packed, amp, energy[:, None, :], energy[:, :, None])


def on_device(atom_blocks, domains, pno_counts, pno_coeffs, amplitudes, pno_energies):
    lane_count = lax.axis_size("ri")
    pair_dev = domains.shape[0]
    mine = pair_products(atom_blocks.transpose(1, 0, 2), domains.T, pno_coeffs, lane_count)
    sub_count = pair_dev // lane_count
    start = lax.axis_index("ri") * sub_count
    counts_here = lax.dynamic_slice_in_dim(pno_counts, start, sub_count, 0)
    return tail(counts_here, mine, amplitudes, pno_energies)


def solution(mesh):
    placed = (
        P("pairs", None, "ri"),
        P("pairs", None),
        P("pairs"),
        P("pairs", None, None),
        P(("pairs", "ri"), None, None),
        P(("pairs", "ri"), None),
    )
    return jax.shard_map(
        on_device,
        mesh=mesh,
        in_specs=placed,
        out_specs=P(("pairs", "ri"), None, None),
        check_vma=False,
    )
```

time: 565 us -> 111 us (0.20)
  waiting for transfers between devices: 197 us -> 0 us
  local copies, waits for them, and re-layouts: 194 us -> 2.68 us
  Pallas kernels: 0 us -> 108 us
  matrix products: 99.1 us -> 0 us
  other arithmetic: 36.3 us -> 0 us
  blocking collectives: 15.3 us -> 0 us
  between operations: 13.5 us -> 0.04 us
  starting transfers between devices: 5.97 us -> 0 us
    gather x34 -> x0, local copies, waits for them, and re-layouts: 165 us -> none  [the longest x32 127 us: vectors_of(): jnp.take(received, item[1], axis=0).reshape(domain_size * band, aux_cols)]
    pallas_call x0 -> x2, Pallas kernels: none -> 108 us  [the longest x1 105 us: pair_products(): pl.pallas_call(main_kernel, out_shape=jax.ShapeDtypeStruct((2, DUO, LANES...]
    dot_general x33 -> x0, matrix products: 99.1 us -> none  [the longest x32 96 us: partial_products(): return jnp.dot(vectors, vectors.T, preferred_element_type=jnp.float32)]
    reduce_scatter x1 -> x0, waiting for transfers between devices: 98.9 us -> none  [on_device(): lax.psum_scatter(terms, 'ri', scatter_dimension=0, tiled=True) / NAUX]
    all_to_all x1 -> x0, waiting for transfers between devices: 97.7 us -> none  [on_device(): lax.all_to_all(picked, 'pairs', split_axis=0, concat_axis=0, tiled=True)]
    lt x33 -> x0, other arithmetic: 21.8 us -> none  [the longest x32 21.7 us: project(): valid = jnp.arange(slot_count, dtype=jnp.int32) < count]
    dynamic_slice x32 -> x0, local copies, waits for them, and re-layouts: 21.1 us -> none  [on_device(): terms = lax.map(partial_products, (pno_coeffs, slot_rows, pno_counts))]
    all_to_all x1 -> x0, blocking collectives: 15.3 us -> none  [on_device(): lax.all_to_all(requests, 'pairs', split_axis=0, concat_axis=0, tiled=True)]
  transfers between devices with their start and end apart: 2 -> 0, of which waited for: 2 -> 0; matrix products, arithmetic and copies ran while one was open for 0% -> 0% of each run, Pallas kernels for 0% -> 0%
where the time goes in v1:
time: 111 us; the launch traced here: 110 us
  Pallas kernels  108 us (97%)
  local copies, waits for them, and re-layouts  2.68 us (2%)
    pallas_call x1, Pallas kernels, pair_products(): pl.pallas_call(main_kernel, out_shape=jax.ShapeDtypeStruct((2, DUO, LANES...  105 us
    pallas_call x1, Pallas kernels, tail(): pl.pallas_call(tail_kernel, out_shape=jax.ShapeDtypeStruct((subs, slots,...  2.43 us

profile of v1, /device:TPU:1, one launch (start us, length us, event | category | flops | bytes accessed | tf_op | source)
XLA Modules:
  0.0 110.4 jit_solution(2103764932776926876)
XLA Ops:
  0.0 0.0 copy-start.2
  0.0 0.0 copy-start.1
  0.0 0.8 dynamic_slice.3.counts
  0.8 0.7 broadcast_in_dim.6.energy_row
  1.5 105.3 %shard_map.64.packed = f32[2,352,128]{2,1,0:T(8,128)} custom-call(bf16[20,16,1792]{2,1,0:T(8,128)(2,1)} %bitcast.3, s32[12,32]{1,0:T(8,128)} %bitcast.5, bf16[32,240,256]{2,1,0:T(8,128)(2,1)} %coeff_hbm.1), custom_call_target="tpu_custom_call" | custom-call | tf_op jit(solution)/shard_map/pallas_call | solution.py:555
  106.8 0.0 copy-done.2
  106.8 0.2 copy.7.energy_col
  107.0 0.0 copy-done.1
  107.0 0.0 copy-start
  107.0 1.0 copy-done
  108.0 2.4 %shard_map.65 = f32[4,256,256]{2,1,0:T(8,128)} custom-call(s32[4]{0:T(128)S(1)} %dynamic_slice.3.counts, f32[2,352,128]{2,1,0:T(8,128)S(1)} %copy-done, bf16[4,256,256]{2,1,0:T(8,128)(2,1)S(1)} %copy-done.1, f32[4,1,256]{2,1,0:T(1,128)S(1)} %broadcast_in_dim.6.energy_row, f32[4,256,1]{2,1,0:T(8,128)S(1)} %copy.7.energy_col), custom_call_target="tpu_custom_call" | custom-call | tf_op jit(solution)/shard_map/pallas_call | solution.py:615
Async XLA Ops:
  0.0 106.8 %copy-start.2 = (f32[4,256]{1,0:T(4,128)S(1)}, f32[4,256]{1,0:T(4,128)}, u32[]{:S(2)}) copy-start(f32[4,256]{1,0:T(4,128)} %param.11) | copy-start | bytes 12292
  0.0 107.0 %copy-start.1 = (bf16[4,256,256]{2,1,0:T(8,128)(2,1)S(1)}, bf16[4,256,256]{2,1,0:T(8,128)(2,1)}, u32[]{:S(2)}) copy-start(bf16[4,256,256]{2,1,0:T(8,128)(2,1)} %amp.1) | copy-start | bytes 1572868
  107.0 1.0 copy-start

commit v2 on v1

--- a/solution.py
+++ b/solution.py
@@ -23,17 +23,19 @@
 HALF = PICKS // 2
 DEPTH = 256
 DUO = SPLIT + 3 * REST + 8
-TILES = (4, 4, 3, 3)
-FIRST = (0, 4, 8, 11)
+COUNTS = DUO - 6
+SLOTS = 48
+SHARE = SLOTS // CORES
+HALF_SHARE = SHARE // 2
+ROW_LINES = RING * CORES
+MAINS = ((0, 1, 2), (3, 4, 5), (6, 7, 8), (10, 11, 12))
+RESTS = ((0, 1, 2), (3, 4, 5), (6, 7, 8, 9), (10, 11, 12, 13))
+SINGLES = (9, 13)
 MESH = pl.DeviceIdType.MESH
 
 
 def params(mib, **kw):
     return pltpu.CompilerParams(vmem_limit_bytes=mib * MIB, **kw)
-
-
-def widths(chunk):
-    return TILES[chunk] * LANES, TILES[chunk] * LANES + LANES
 
 
 class Ports:
@@ -153,13 +155,196 @@
             copy.wait_send()
 
 
+class Relay:
+    def __init__(self, chunk, first_to, other_to, u, v, core, bufs, out_sems, in_sems):
+        self.chunk, self.first_to, self.other_to = chunk, first_to, other_to
+        self.u, self.v, self.core = u, v, core
+        self.wire, self.table, self.passing, self.send, self.relay, self.recv = bufs
+        self.out_sems, self.in_sems = out_sems, in_sems
+
+    def copy(self, src, dst, out_at, in_at, to):
+        return pltpu.make_async_remote_copy(
+            src_ref=src,
+            dst_ref=dst,
+            send_sem=self.out_sems.at[self.chunk, out_at],
+            recv_sem=self.in_sems.at[self.chunk, in_at],
+            device_id={"pairs": to},
+            device_id_type=MESH,
+        )
+
+    def arrival(self, dst, at):
+        return self.copy(dst, dst, at, at, self.first_to(1, self.core))
+
+    def near_u(self, step):
+        return lax.rem(self.u + step, RING)
+
+    def near_v(self, step):
+        return lax.rem(self.v + step, RING)
+
+    def atoms(self, step, at=0, count=ATOMS):
+        base = ((self.v * CORES + self.core) * RING + self.near_u(step)) * ATOMS
+        return self.table.at[pl.ds(base + at, count)]
+
+    def block(self, step, core, at=0, count=RING * ATOMS):
+        return self.table.at[pl.ds((self.near_v(step) * CORES + core) * RING * ATOMS + at, count)]
+
+    def spread_sends(self):
+        half = ATOMS // 2
+        far = self.near_u(2)
+        up, down = self.first_to(1, self.core), self.first_to(3, self.core)
+        return [
+            self.copy(self.wire.at[far, pl.ds(0, half)], self.passing.at[0], 2, 2, up),
+            self.copy(self.wire.at[far, pl.ds(half, half)], self.passing.at[1], 3, 3, down),
+            self.copy(self.wire.at[self.near_u(1)], self.atoms(0), 0, 1, up),
+            self.copy(self.wire.at[self.near_u(3)], self.atoms(0), 1, 0, down),
+        ]
+
+    def spread_own(self):
+        return pltpu.make_async_copy(self.wire.at[self.u], self.atoms(0), self.in_sems.at[self.chunk, 25])
+
+    def spread_onward(self):
+        half = ATOMS // 2
+        return [
+            self.copy(self.passing.at[0], self.atoms(3, 0, half), 4, 4, self.first_to(1, self.core)),
+            self.copy(self.passing.at[1], self.atoms(1, half, half), 5, 5, self.first_to(3, self.core)),
+        ]
+
+    def start_spread(self):
+        for copy in self.spread_sends():
+            copy.start()
+        self.spread_own().start()
+
+    def forward_spread(self):
+        for way, copy in enumerate(self.spread_onward()):
+            self.arrival(self.passing.at[way], 2 + way).wait_recv()
+            copy.start()
+
+    def finish_spread(self):
+        half = ATOMS // 2
+        self.spread_own().wait()
+        self.arrival(self.atoms(1), 0).wait_recv()
+        self.arrival(self.atoms(3), 1).wait_recv()
+        self.arrival(self.atoms(2, 0, half), 4).wait_recv()
+        self.arrival(self.atoms(2, half, half), 5).wait_recv()
+
+    def gather_first(self):
+        own = self.block(0, self.core)
+        return [
+            self.copy(own, own, 6, 7, self.other_to(1, self.core)),
+            self.copy(own, own, 7, 6, self.other_to(3, self.core)),
+        ]
+
+    def gather_second(self):
+        half = RING * ATOMS // 2
+        low, high = self.block(3, self.core, 0, half), self.block(1, self.core, half, half)
+        return [
+            self.copy(low, low, 8, 8, self.other_to(1, self.core)),
+            self.copy(high, high, 9, 9, self.other_to(3, self.core)),
+        ]
+
+    def share(self, step):
+        mine = self.block(step, self.core)
+        return self.copy(mine, mine, 10 + step, 10 + step, self.first_to(0, 1 - self.core))
+
+    def start_gather(self):
+        for copy in self.gather_first():
+            copy.start()
+        self.share(0).start()
+
+    def forward_gather(self):
+        low, high = self.gather_second()
+        self.arrival(self.block(3, self.core), 7).wait_recv()
+        low.start()
+        self.share(3).start()
+        self.arrival(self.block(1, self.core), 6).wait_recv()
+        high.start()
+        self.share(1).start()
+
+    def finish_gather(self):
+        half = RING * ATOMS // 2
+        self.arrival(self.block(2, self.core, 0, half), 8).wait_recv()
+        self.arrival(self.block(2, self.core, half, half), 9).wait_recv()
+        self.share(2).start()
+
+    def finish_share(self):
+        for step in range(RING):
+            self.arrival(self.block(step, 1 - self.core), 10 + step).wait_recv()
+
+    def place(self, step, core, at=0, count=SHARE):
+        return self.recv.at[self.near_u(step), pl.ds(core * SHARE + at, count)]
+
+    def far(self):
+        return [
+            self.copy(self.send.at[2, :, pl.ds(0, HALF_SHARE)], self.relay.at[0], 19, 19, self.first_to(1, self.core)),
+            self.copy(
+                self.send.at[2, :, pl.ds(HALF_SHARE, HALF_SHARE)], self.relay.at[1], 20, 20, self.first_to(3, self.core)
+            ),
+        ]
+
+    def near(self):
+        copies = []
+        dst = self.place(0, self.core)
+        for n, step in enumerate((1, 3)):
+            for core in range(CORES):
+                at = 14 + 2 * n
+                copies.append(self.copy(self.send.at[step, core], dst, at + core, at + self.core, self.first_to(step, core)))
+        other = 1 - self.core
+        copies.append(self.copy(self.send.at[0, other], dst, 18, 18, self.first_to(0, other)))
+        return copies
+
+    def own(self):
+        return pltpu.make_async_copy(
+            self.send.at[0, self.core], self.place(0, self.core), self.in_sems.at[self.chunk, 26]
+        )
+
+    def onward(self):
+        copies = []
+        for way, step in enumerate((1, 3)):
+            dst = self.place(RING - step, self.core, way * HALF_SHARE, HALF_SHARE)
+            for core in range(CORES):
+                at = 21 + 2 * way
+                copies.append(self.copy(self.relay.at[way, core], dst, at + core, at + self.core, self.first_to(step, core)))
+        return copies
+
+    def start_delivery(self):
+        for copy in self.far() + self.near():
+            copy.start()
+        self.own().start()
+
+    def forward_delivery(self):
+        onward = self.onward()
+        for way in range(2):
+            self.arrival(self.relay.at[way], 19 + way).wait_recv()
+            for copy in onward[2 * way : 2 * way + 2]:
+                copy.start()
+
+    def finish_delivery(self):
+        for core in range(CORES):
+            self.arrival(self.place(3, core), 14 + core).wait_recv()
+            self.arrival(self.place(1, core), 16 + core).wait_recv()
+            for way in range(2):
+                at = 21 + 2 * way + core
+                self.arrival(self.place(2, core, way * HALF_SHARE, HALF_SHARE), at).wait_recv()
+        self.arrival(self.place(0, 1 - self.core), 18).wait_recv()
+        self.own().wait()
+
+    def finish_sends(self):
+        copies = self.spread_sends() + self.spread_onward() + self.gather_first() + self.gather_second()
+        copies += [self.share(step) for step in range(RING)] + self.far() + self.near() + self.onward()
+        for copy in copies:
+            copy.wait_send()
+
+
 def main_kernel(
-    blocks, domains, coeff_hbm, out, *scratch
+    blocks, domains, counts, coeff_hbm, out, *scratch
 ):
-    wires, rings, sends, relays, recvs = (scratch[4 * n : 4 * n + 4] for n in range(5))
-    asked, asked_smem, tables, places, request, ids, perm_main, perm_rest = scratch[20:28]
-    coeff, coeff_t, perm, blk, total, sums, fresh = scratch[28:35]
-    out_sems, in_sems, ask_out, ask_in, local_sems, sum_out, sum_in = scratch[35:42]
+    relay_bufs = [scratch[4 * n : 4 * n + 4] for n in range(6)]
+    single_bufs = [scratch[24 + 2 * n : 26 + 2 * n] for n in range(5)]
+    wires, recvs = relay_bufs[0], relay_bufs[5]
+    single_wires, single_recvs = single_bufs[0], single_bufs[4]
+    asked, asked_smem, tables, places, request, ids, perm_main, perm_rest = scratch[34:42]
+    coeff, coeff_t, perm, blk, total, sums, fresh, same = scratch[42:50]
+    out_sems, in_sems, single_out, single_in, ask_out, ask_in, local_sems, sum_out, sum_in = scratch[50:59]
     me = lax.axis_index("pairs")
     at_z = lax.axis_index("ri")
     planes = 2 * (sums.shape[1] - 1)
@@ -205,36 +390,53 @@
 
     ports = []
     for chunk in range(4):
-        gather_to, deliver_to = (along_x, along_y) if chunk % 2 == 0 else (along_y, along_x)
-        ports.append(
-            Ports(
-                chunk, gather_to, deliver_to, wires[chunk], rings[chunk], sends[chunk],
-                relays[chunk], recvs[chunk], out_sems, in_sems, core,
-            )
-        )
+        by_x = chunk % 2 == 0
+        first_to, other_to = (along_x, along_y) if by_x else (along_y, along_x)
+        u, v = (at_x, at_y) if by_x else (at_y, at_x)
+        bufs = [group_bufs[chunk] for group_bufs in relay_bufs]
+        ports.append(Relay(chunk, first_to, other_to, u, v, core, bufs, out_sems, in_sems))
+    singles = []
+    for n in range(2):
+        gather_to, deliver_to = (along_x, along_y) if n == 0 else (along_y, along_x)
+        bufs = [group_bufs[n] for group_bufs in single_bufs]
+        singles.append(Ports(n, gather_to, deliver_to, *bufs, single_out, single_in, core))
 
     square = (ATOMS * MAIN, ATOMS * MAIN)
     out_at = lax.broadcasted_iota(jnp.int32, square, 0)
     from_at = lax.broadcasted_iota(jnp.int32, square, 1)
-    band_at, atom_at = out_at % MAIN, out_at // MAIN
+    band_at, atom_at = out_at & (MAIN - 1), lax.shift_right_logical(out_at, 4)
     perm_main[...] = jnp.where(band_at * ATOMS + atom_at == from_at, 1.0, 0.0).astype(jnp.bfloat16)
-    rest_at = (band_at // REM) * (REM * ATOMS) + (band_at % REM) * ATOMS + atom_at
+    rest_at = lax.shift_right_logical(band_at, 2) * (REM * ATOMS) + (band_at & (REM - 1)) * ATOMS + atom_at
     perm_rest[...] = jnp.where(rest_at == from_at, 1.0, 0.0).astype(jnp.bfloat16)
 
+    def main_rows(tiles):
+        flat = blocks[:MAIN, :, tiles[0] * LANES : (tiles[-1] + 1) * LANES]
+        flat = flat.reshape(MAIN * ATOMS, len(tiles) * LANES)
+        return jnp.dot(perm_main[...], flat, preferred_element_type=jnp.float32).astype(jnp.bfloat16)
+
     def form(chunk):
-        cols, _ = widths(chunk)
-        begin = FIRST[chunk] * LANES
-        flat = blocks[:MAIN, :, begin : begin + cols].reshape(MAIN * ATOMS, cols)
-        main = jnp.dot(perm_main[...], flat, preferred_element_type=jnp.float32).astype(jnp.bfloat16)
-        wires[chunk][:, :, :cols] = main.reshape(ATOMS, MAIN, cols)
-        rest = blocks[MAIN:, :, begin : begin + cols].reshape(REM * ATOMS, cols)
-        stacked = jnp.concatenate([rest[:, q * LANES : (q + 1) * LANES] for q in range(TILES[chunk])], axis=0)
+        main = main_rows(MAINS[chunk])
+        for n in range(len(MAINS[chunk])):
+            wires[chunk][n] = main[:, n * LANES : (n + 1) * LANES].reshape(ATOMS, MAIN, LANES)
+        parts = [blocks[MAIN:, :, t * LANES : (t + 1) * LANES].reshape(REM * ATOMS, LANES) for t in RESTS[chunk]]
+        stacked = jnp.concatenate(parts, axis=0)
         depth = stacked.shape[0]
         late = jnp.dot(perm_rest[:, :depth], stacked, preferred_element_type=jnp.float32).astype(jnp.bfloat16)
-        wires[chunk][:, :, cols:] = late.reshape(ATOMS, MAIN, LANES)
+        wires[chunk][RING - 1] = late.reshape(ATOMS, MAIN, LANES)
 
     form(0)
-    form(1)
+    pl.semaphore_wait(barrier, len(peers) + 2)
+    ports[0].start_spread()
+    for chunk in range(1, 4):
+        form(chunk)
+        ports[chunk].start_spread()
+    for n in range(2):
+        single_wires[n][...] = main_rows(SINGLES[n : n + 1]).reshape(ATOMS, MAIN, LANES)
+    for chunk in (0, 1):
+        ports[chunk].forward_spread()
+    for chunk in (0, 1):
+        ports[chunk].finish_spread()
+        ports[chunk].start_gather()
 
     ids[...] = jnp.zeros_like(ids)
     pairs = domains.shape[1]
@@ -257,35 +459,47 @@
     for line in lines:
         named = jnp.where(atom == line, 1, named)
     named = jnp.broadcast_to(jnp.max(named, axis=1, keepdims=True), flat_shape)
-    local = atom % ATOMS
-    owner = atom // ATOMS
+    local = atom & (ATOMS - 1)
+    owner = lax.shift_right_logical(atom, 4)
     rank = named
     for shift in (1, 2, 4, 8):
         rank = rank + jnp.where(local >= shift, pltpu.roll(rank, shift, 0), 0)
+    order = named
+    for shift in (1, 2, 4, 8, 16, 32, 64, 128, 256):
+        order = order + jnp.where(atom >= shift, pltpu.roll(order, shift, 0), 0)
     own_lane = jnp.where((owner == lane_at) & (named > 0), local, 0)
     for j in range(CAP):
         request[j : j + 1, :] = jnp.sum(jnp.where(rank == j + 1, own_lane, 0), axis=0, keepdims=True)
-    request[CAP:, :] = jnp.zeros((8 - CAP, LANES), jnp.int32)
-
-    pl.semaphore_wait(barrier, len(peers) + 2)
-    ports[0].start_gather()
-    ports[1].start_gather()
+    owner_chip = lax.shift_right_logical(owner, 1)
+    owner_core = owner & (CORES - 1)
+    owner_x, owner_y = owner_chip & (RING - 1), lax.shift_right_logical(owner_chip, 2)
+    taken = (order == lane_at + 1) & (named > 0)
+    for n, (u, v) in enumerate(((owner_x, owner_y), (owner_y, owner_x))):
+        held_at = ((v * CORES + owner_core) * RING + u) * ATOMS + local
+        request[CAP + n : CAP + n + 1, :] = jnp.sum(jnp.where(taken, held_at, 0), axis=0, keepdims=True)
+    request[CAP + 2 :, :] = jnp.zeros((6 - CAP, LANES), jnp.int32)
+
     for n in range(len(peers)):
         ask(n).start()
     own_ask = pltpu.make_async_copy(request, asked.at[core], local_sems.at[1])
     own_ask.start()
 
-    form(2)
-    form(3)
-    owner_chip = owner // CORES
-    rel_x = (owner_chip + RING - at_x) % RING
-    rel_y = (owner_chip // RING + RING - at_y) % RING
-    owner_core = owner % CORES
+    for chunk in (2, 3):
+        ports[chunk].forward_spread()
+    for chunk in (2, 3):
+        ports[chunk].finish_spread()
+    for chunk in (0, 1):
+        ports[chunk].forward_gather()
+    for chunk in (2, 3):
+        ports[chunk].start_gather()
+
+    rel_x = (owner_x + RING - at_x) & (RING - 1)
+    rel_y = (owner_y + RING - at_y) & (RING - 1)
     place_x = ((rel_y * CORES + owner_core) * RING + rel_x) * CAP + rank - 1
     place_y = ((rel_x * CORES + owner_core) * RING + rel_y) * CAP + rank - 1
     tables[...] = jnp.zeros_like(tables)
     for n, line in enumerate(lines):
-        for table, place in enumerate((place_x, place_y)):
+        for table, place in enumerate((order - 1, place_x, place_y)):
             tables[table, n : n + 1, :] = jnp.sum(jnp.where(atom == line, place, 0), axis=0, keepdims=True)
     table_copy = pltpu.make_async_copy(tables, places, local_sems.at[3])
     table_copy.start()
@@ -302,26 +516,33 @@
         (late // REM) * BAND + MAIN + late % REM,
     )
     perm[...] = jnp.where((source == col) & (row < DOM * BAND), 1.0, 0.0).astype(jnp.bfloat16)
+    same[...] = jnp.where(
+        lax.broadcasted_iota(jnp.int32, same.shape, 0) == lax.broadcasted_iota(jnp.int32, same.shape, 1), 1.0, 0.0
+    ).astype(jnp.bfloat16)
     for n in range(2):
         blk[n, DOM * BAND :, :] = jnp.zeros((DEPTH - DOM * BAND, blk.shape[2]), jnp.bfloat16)
     fetch.wait()
 
     def prepare(begin, end):
         def turn(pair, _):
-            ordered = jnp.dot(perm[...], coeff[pair], preferred_element_type=jnp.float32)
-            coeff_t[pair] = ordered.T[:MAXPNO].astype(jnp.bfloat16)
+            ordered = [
+                jnp.dot(perm[...], coeff[4 * pair + n], preferred_element_type=jnp.float32).astype(jnp.bfloat16)
+                for n in range(4)
+            ]
+            for n in range(4):
+                turned = lax.dot_general(
+                    same[...], ordered[n], (((1,), (1,)), ((), ())), preferred_element_type=jnp.float32
+                )
+                coeff_t[4 * pair + n] = turned.astype(jnp.bfloat16)
             return 0
 
-        lax.fori_loop(begin, end, turn, 0)
+        lax.fori_loop(begin // 4, end // 4, turn, 0)
 
     half_pairs = coeff.shape[0] // 2
     quarter = half_pairs // 2
-    prepare(0, half_pairs - REM)
-    ports[0].forward_gather()
-    ports[1].forward_gather()
-    ports[2].start_gather()
-    ports[3].start_gather()
-    prepare(half_pairs - REM, half_pairs + REM)
+    for single in singles:
+        single.start_gather()
+    prepare(0, quarter)
 
     own_ask.wait()
     for n in range(len(peers)):
@@ -338,12 +559,15 @@
     to_smem.start()
     to_smem.wait()
 
-    def pick(chunk):
-        port = ports[chunk]
-        owner_of = along_x if chunk % 2 == 0 else along_y
+    def line_of(dest, on_row):
+        return jnp.where(dest < CORES, dest, dest + ROW_LINES) if on_row else dest
+
+    def pick_single(n):
+        port = singles[n]
+        owner_of = along_x if n == 0 else along_y
 
         def serve(dest, _):
-            line = dest if chunk % 2 == 0 else jnp.where(dest < CORES, dest, dest + RING * CORES)
+            line = line_of(dest, n == 1)
             step, to_core = dest // CORES, dest % CORES
             for r in range(RING):
                 for j in range(CAP):
@@ -354,22 +578,44 @@
 
         lax.fori_loop(0, RING * CORES, serve, 0)
 
+    def pick(chunk):
+        port = ports[chunk]
+
+        def serve(dest, _):
+            line = line_of(dest, chunk % 2 == 0)
+            step, to_core = dest // CORES, dest % CORES
+            for n in range(SHARE):
+                port.send[step, to_core, n] = port.table[asked_smem[line, CAP + chunk % 2, core * SHARE + n]]
+            return 0
+
+        lax.fori_loop(0, RING * CORES, serve, 0)
+
     for chunk in (0, 1):
         ports[chunk].finish_gather()
+    for chunk in (0, 1):
+        ports[chunk].finish_share()
         pick(chunk)
         ports[chunk].start_delivery()
     for chunk in (2, 3):
         ports[chunk].forward_gather()
-    prepare(half_pairs + REM, half_pairs + quarter)
-    ports[0].forward_delivery()
-    ports[1].forward_delivery()
+    for single in singles:
+        single.forward_gather()
+    prepare(quarter, half_pairs)
+    for chunk in (0, 1):
+        ports[chunk].forward_delivery()
     for chunk in (2, 3):
         ports[chunk].finish_gather()
+    for n in range(2):
+        singles[n].finish_gather()
+        pick_single(n)
+        singles[n].start_delivery()
+    for chunk in (2, 3):
+        ports[chunk].finish_share()
         pick(chunk)
-    prepare(half_pairs + quarter, 2 * half_pairs)
-    for chunk in (2, 3):
-        ports[chunk - 2].finish_served()
         ports[chunk].start_delivery()
+    for single in singles:
+        single.forward_delivery()
+    prepare(half_pairs, 2 * half_pairs)
 
     pack_row = lax.broadcasted_iota(jnp.int32, (SPLIT, LANES), 0)
     pack_col = lax.broadcasted_iota(jnp.int32, (SPLIT, LANES), 1)
@@ -379,25 +625,36 @@
     def assemble(pair, slot, chunks):
         base = MAIN * DOM
         begin = 0
-        for table, chunk in enumerate(chunks):
-            cols, _ = widths(chunk)
-            upper = lax.broadcasted_iota(jnp.int32, (8, LANES), 0) < REM
-            at = [places[table, k // fold, (k % fold) * pairs + pair] for k in range(DOM)]
-            for k in range(DOM):
-                blk[slot, MAIN * k : MAIN * (k + 1), begin : begin + cols] = recvs[chunk][at[k], :, :cols]
+        upper = lax.broadcasted_iota(jnp.int32, (8, LANES), 0) < REM
+
+        def named_at(table):
+            return [places[table, k // fold, (k % fold) * pairs + pair] for k in range(DOM)]
+
+        at = named_at(0)
+        for chunk in chunks:
+            tiles = len(RESTS[chunk])
+            for n in range(RING - 1):
+                span = slice(begin + n * LANES, begin + (n + 1) * LANES)
+                for k in range(DOM):
+                    blk[slot, MAIN * k : MAIN * (k + 1), span] = recvs[chunk][n, at[k]]
+            if tiles == RING:
+                span = slice(begin + (RING - 1) * LANES, begin + RING * LANES)
+                single_at = named_at(1 + chunk % 2)
+                for k in range(DOM):
+                    blk[slot, MAIN * k : MAIN * (k + 1), span] = single_recvs[chunk % 2][single_at[k]]
             for k in range(0, DOM, 4):
-                rest = [recvs[chunk][at[k + n], :, cols:].astype(jnp.float32) for n in range(4)]
-                for half in range((TILES[chunk] + 1) // 2):
+                rest = [recvs[chunk][RING - 1, at[k + n]].astype(jnp.float32) for n in range(4)]
+                for half in range((tiles + 1) // 2):
                     parts = [r[8 * half : 8 * half + 8] for r in rest]
                     shifted = [pltpu.roll(part, REM, 0) for part in parts]
-                    for q in range(2 * half, min(2 * half + 2, TILES[chunk])):
+                    for q in range(2 * half, min(2 * half + 2, tiles)):
                         first, second = (parts, shifted) if q % 2 == 0 else (shifted, parts)
                         low = jnp.where(upper, first[0], second[1])
                         high = jnp.where(upper, first[2], second[3])
                         both = jnp.concatenate([low, high], axis=0).astype(jnp.bfloat16)
                         tile = slice(begin + q * LANES, begin + (q + 1) * LANES)
                         blk[slot, base + REM * k : base + REM * (k + 4), tile] = both
-            begin += cols
+            begin += tiles * LANES
         return begin
 
     def multiply(pair, slot, cols):
@@ -410,12 +667,15 @@
         return result
 
     def first_half(step, _):
-        for n in range(2):
-            cols = assemble(2 * step + n, n, (0, 1))
-        for n in range(2):
-            total[2 * step + n] = multiply(2 * step + n, n, cols)
+        pair = 2 * step
+        assemble(pair + 1, 1, (0, 1))
+        total[pair] = multiply(pair, 0, early_cols)
+        assemble(jnp.minimum(pair + 2, coeff.shape[0] - 1), 0, (0, 1))
+        total[pair + 1] = multiply(pair + 1, 1, early_cols)
         return 0
 
+    early_cols = LANES * (len(RESTS[0]) + len(RESTS[1]))
+    late_cols = LANES * (len(RESTS[2]) + len(RESTS[3]))
     group = coeff.shape[0] // planes
     half_ring = planes // 2
     part = DUO // 2
@@ -431,11 +691,29 @@
             device_id_type=MESH,
         )
 
-    def second_half(owner, duo):
-        first = owner * group + 2 * duo
-        for n in range(2):
-            cols = assemble(first + n, n, (2, 3))
-        whole = [total[first + n] + multiply(first + n, n, cols) for n in range(2)]
+    sends = 2 + 4 * (half_ring - 1)
+
+    def locate(item):
+        later = jnp.clip(item - 2, 0, sends - 3)
+        turn = later % 4
+        opening = item < 2
+        step = jnp.where(opening, 0, 1 + later // 4)
+        way = jnp.where(opening, item, turn % 2)
+        early = jnp.logical_and(jnp.logical_not(opening), turn < 2)
+        duo = jnp.where(early, 1 - way, way)
+        away = jnp.where(way == 0, half_ring - step, half_ring + step)
+        mine = item >= sends
+        duo = jnp.where(mine, jnp.minimum(item - sends, 1), duo)
+        owner = jnp.where(mine, at_z, lax.rem(at_z + away, planes))
+        alone = jnp.logical_or(opening, jnp.logical_and(early, step == 1))
+        return step, way, duo, owner * group + 2 * duo, alone
+
+    def second_half(item):
+        first, following = locate(item)[3], locate(item + 1)[3]
+        assemble(first + 1, 1, (2, 3))
+        whole = [total[first] + multiply(first, 0, late_cols)]
+        assemble(following, 0, (2, 3))
+        whole.append(total[first + 1] + multiply(first + 1, 1, late_cols))
         here, there = [w[:SPLIT, :SPLIT] for w in whole]
         fresh[:SPLIT, :] = jnp.where(pack_row >= pack_col, here, there)
         for n in range(2):
@@ -450,16 +728,8 @@
         )
 
     def send_on(item, _):
-        later = jnp.maximum(item - 2, 0)
-        turn = later % 4
-        opening = item < 2
-        step = jnp.where(opening, 0, 1 + later // 4)
-        way = jnp.where(opening, item, turn % 2)
-        early = jnp.logical_and(jnp.logical_not(opening), turn < 2)
-        duo = jnp.where(early, 1 - way, way)
-        away = jnp.where(way == 0, half_ring - step, half_ring + step)
-        second_half(lax.rem(at_z + away, planes), duo)
-        alone = jnp.logical_or(opening, jnp.logical_and(early, step == 1))
+        step, way, duo, _, alone = locate(item)
+        second_half(item)
 
         @pl.when(alone)
         def _():
@@ -478,61 +748,75 @@
         return 0
 
     def send_done(item, _):
-        later = jnp.maximum(item - 2, 0)
-        turn = later % 4
-        opening = item < 2
-        step = jnp.where(opening, 0, 1 + later // 4)
-        way = jnp.where(opening, item, turn % 2)
-        early = jnp.logical_and(jnp.logical_not(opening), turn < 2)
-        duo = jnp.where(early, 1 - way, way)
+        step, way, duo, _, _ = locate(item)
         for piece in range(2):
             chain(way, step, duo, piece).wait_send()
         return 0
 
     ports[0].finish_delivery()
     ports[1].finish_delivery()
-    lax.fori_loop(0, half_pairs // 2, first_half, 0)
+    assemble(0, 0, (0, 1))
+    lax.fori_loop(0, half_pairs // 4, first_half, 0)
     ports[2].forward_delivery()
     ports[3].forward_delivery()
-    lax.fori_loop(half_pairs // 2, half_pairs, first_half, 0)
+    lax.fori_loop(half_pairs // 4, half_pairs, first_half, 0)
+    for single in singles:
+        single.finish_delivery()
     ports[2].finish_delivery()
     ports[3].finish_delivery()
     fresh[...] = jnp.zeros_like(fresh)
-    items = 2 + 4 * (half_ring - 1)
-    lax.fori_loop(0, items, send_on, 0)
+    assemble(locate(0)[3], 0, (2, 3))
+    lax.fori_loop(0, sends, send_on, 0)
     for duo in range(2):
-        second_half(at_z, duo)
+        second_half(sends + duo)
         for piece in range(2):
             rows = slice(piece * part, (piece + 1) * part)
             for way in range(2):
                 chain(way, half_ring - 1, duo, piece).wait_recv()
             arrived = sums[0, half_ring, duo, rows, :] + sums[1, half_ring, duo, rows, :]
             out[duo, rows, :] = arrived + fresh[rows, :]
-    lax.fori_loop(0, items, send_done, 0)
-    for chunk in (2, 3):
-        ports[chunk].finish_served()
+        for n in range(2):
+            count = counts[at_z * group + 2 * duo + n].astype(jnp.float32)
+            out[duo, COUNTS + n : COUNTS + n + 1, :] = jnp.full((1, LANES), count)
+    lax.fori_loop(0, sends, send_done, 0)
     for n in range(len(peers)):
         ask(n).wait_send()
-    for chunk in range(4):
-        ports[chunk].finish_sends()
-
-
-def pair_products(blocks, domains, coeff, planes):
+    for port in ports:
+        port.finish_sends()
+    for single in singles:
+        single.finish_served()
+        single.finish_sends()
+
+
+def pair_products(blocks, domains, counts, coeff, planes):
     pair_dev, depth, slots = coeff.shape
     lines = 2 * RING * CORES
-    wide = [widths(chunk)[1] for chunk in range(4)]
-    half_cols = widths(0)[0] + widths(1)[0]
+    half_cols = RING * LANES * 2
     bf16 = jnp.bfloat16
-    scratch = [pltpu.VMEM((ATOMS, MAIN, w), bf16) for w in wide]
-    scratch += [pltpu.VMEM((RING - 1, ATOMS, MAIN, w), bf16) for w in wide]
-    scratch += [pltpu.VMEM((RING, CORES, PICKS, MAIN, w), bf16) for w in wide]
-    scratch += [pltpu.VMEM((2, CORES, HALF, MAIN, w), bf16) for w in wide]
-    scratch += [pltpu.VMEM((RING * CORES * PICKS, MAIN, w), bf16) for w in wide]
+    tile = (MAIN, LANES)
+    scratch = []
+    for shape in (
+        (RING, ATOMS),
+        (RING * RING * CORES * ATOMS,),
+        (2, ATOMS // 2),
+        (RING, CORES, SHARE),
+        (2, CORES, HALF_SHARE),
+        (RING, SLOTS),
+    ):
+        scratch += [pltpu.VMEM(shape + tile, bf16)] * 4
+    for shape in (
+        (ATOMS,),
+        (RING - 1, ATOMS),
+        (RING, CORES, PICKS),
+        (2, CORES, HALF),
+        (RING * CORES * PICKS,),
+    ):
+        scratch += [pltpu.VMEM(shape + tile, bf16)] * 2
     scratch += [
         pltpu.VMEM((lines, 8, LANES), jnp.int32),
         pltpu.SMEM((lines, 8, LANES), jnp.int32),
-        pltpu.VMEM((2, 8, LANES), jnp.int32),
-        pltpu.SMEM((2, 8, LANES), jnp.int32),
+        pltpu.VMEM((3, 8, LANES), jnp.int32),
+        pltpu.SMEM((3, 8, LANES), jnp.int32),
         pltpu.VMEM((8, LANES), jnp.int32),
         pltpu.VMEM((16, LANES), jnp.int32),
         pltpu.VMEM((ATOMS * MAIN, ATOMS * MAIN), bf16),
@@ -544,8 +828,11 @@
         pltpu.VMEM((pair_dev, MAXPNO, MAXPNO), jnp.float32),
         pltpu.VMEM((2, planes // 2 + 1, 2, DUO, LANES), jnp.float32),
         pltpu.VMEM((DUO, LANES), jnp.float32),
-        pltpu.SemaphoreType.DMA((4, 16)),
-        pltpu.SemaphoreType.DMA((4, 16)),
+        pltpu.VMEM((MAXPNO, slots), bf16),
+        pltpu.SemaphoreType.DMA((4, 27)),
+        pltpu.SemaphoreType.DMA((4, 27)),
+        pltpu.SemaphoreType.DMA((2, 16)),
+        pltpu.SemaphoreType.DMA((2, 16)),
         pltpu.SemaphoreType.DMA((lines,)),
         pltpu.SemaphoreType.DMA((lines,)),
         pltpu.SemaphoreType.DMA((4,)),
@@ -558,15 +845,16 @@
         in_specs=[
             pl.BlockSpec(memory_space=pltpu.VMEM),
             pl.BlockSpec(memory_space=pltpu.VMEM),
+            pl.BlockSpec(memory_space=pltpu.SMEM),
             pl.BlockSpec(memory_space=pl.ANY),
         ],
         out_specs=pl.BlockSpec(memory_space=pltpu.VMEM),
         scratch_shapes=scratch,
         compiler_params=params(60, collective_id=0, has_side_effects=True),
-    )(blocks, domains, coeff)
-
-
-def tail_kernel(counts, packed, amp, energy_row, energy_col, out, wide):
+    )(blocks, domains, counts, coeff)
+
+
+def tail_kernel(packed, amp, energy_row, energy_col, out, wide):
     slots = amp.shape[1]
     step = pl.program_id(0)
     row = lax.broadcasted_iota(jnp.int32, (SPLIT, LANES), 0)
@@ -591,7 +879,7 @@
         wide[n, SPLIT : SPLIT + REST, LANES:] = rest
         wide[n, MAXPNO:, :] = jnp.zeros((slots - MAXPNO, slots), jnp.float32)
     for n in range(2):
-        count = counts[2 * step + n]
+        count = packed[0, COUNTS + n : COUNTS + n + 1, :1].astype(jnp.int32)
         held = wide[n]
         products = held + jnp.where(full_row == full_col, 0.0, held.T)
         valid = (full_row < count) & (full_col < count)
@@ -605,38 +893,33 @@
         coupled = lax.dot_general(low, amps, contract, preferred_element_type=jnp.float32)
         coupled += lax.dot_general(mid, amps, contract, preferred_element_type=jnp.float32)
         coupled += lax.dot_general(high, amps, contract, preferred_element_type=jnp.float32)
-        energies = energy_col[n] + energy_row[n]
+        energies = energy_col[n] + energy_row[pl.ds(2 * step + n, 1), :]
         result = products + coupled + energies * amps.astype(jnp.float32)
         out[n] = jnp.where(valid, result, 0.0)
 
 
-def tail(counts, packed, amp, energy):
+def tail(packed, amp, energy):
     subs, slots, _ = amp.shape
     return pl.pallas_call(
         tail_kernel,
         out_shape=jax.ShapeDtypeStruct((subs, slots, slots), jnp.float32),
         grid=(subs // 2,),
         in_specs=[
-            pl.BlockSpec(memory_space=pltpu.SMEM),
             pl.BlockSpec((1, DUO, LANES), lambda i: (i, 0, 0)),
             pl.BlockSpec((2, slots, slots), lambda i: (i, 0, 0)),
-            pl.BlockSpec((2, 1, slots), lambda i: (i, 0, 0)),
+            pl.BlockSpec((subs, slots), lambda i: (0, 0)),
             pl.BlockSpec((2, slots, 1), lambda i: (i, 0, 0)),
         ],
         out_specs=pl.BlockSpec((2, slots, slots), lambda i: (i, 0, 0)),
         scratch_shapes=[pltpu.VMEM((2, slots, slots), jnp.float32)],
         compiler_params=params(32),
-    )(counts, packed, amp, energy[:, None, :], energy[:, :, None])
+    )(packed, amp, energy, energy[:, :, None])
 
 
 def on_device(atom_blocks, domains, pno_counts, pno_coeffs, amplitudes, pno_energies):
-    lane_count = lax.axis_size("ri")
-    pair_dev = domains.shape[0]
-    mine = pair_products(atom_blocks.transpose(1, 0, 2), domains.T, pno_coeffs, lane_count)
-    sub_count = pair_dev // lane_count
-    start = lax.axis_index("ri") * sub_count
-    counts_here = lax.dynamic_slice_in_dim(pno_counts, start, sub_count, 0)
-    return tail(counts_here, mine, amplitudes, pno_energies)
+    planes = lax.axis_size("ri")
+    mine = pair_products(atom_blocks.transpose(1, 0, 2), domains.T, pno_counts, pno_coeffs, planes)
+    return tail(mine, amplitudes, pno_energies)
 
 
 def solution(mesh):

time: 111 us -> 107 us (0.964)
  Pallas kernels: 108 us -> 105 us
  local copies, waits for them, and re-layouts: 2.68 us -> 1.21 us
    pallas_call x1, Pallas kernels: 105 us -> 103 us  [pair_products(): pl.pallas_call(main_kernel, out_shape=jax.ShapeDtypeStruct((2, DUO, LANES...]
where the time goes in v2:
time: 107 us; the launch traced here: 106 us
  Pallas kernels  105 us (98%)
  local copies, waits for them, and re-layouts  1.21 us (1%)
    pallas_call x1, Pallas kernels, pair_products(): pl.pallas_call(main_kernel, out_shape=jax.ShapeDtypeStruct((2, DUO, LANES...  103 us

profile of v2, /device:TPU:1, one launch (start us, length us, event | category | flops | bytes accessed | tf_op | source)
XLA Modules:
  0.0 106.4 jit_solution(10572210142750652230)
XLA Ops:
  0.0 0.0 copy-start.2
  0.0 0.0 copy-start.1
  0.0 103.3 %shard_map.64.packed = f32[2,352,128]{2,1,0:T(8,128)} custom-call(bf16[20,16,1792]{2,1,0:T(8,128)(2,1)} %bitcast.4, s32[12,32]{1,0:T(8,128)} %bitcast.5, s32[32]{0:T(128)} %counts.1, bf16[32,240,256]{2,1,0:T(8,128)(2,1)} %coeff_hbm.1), custom_call_target="tpu_custom_call" | custom-call | tf_op jit(solution)/shard_map/pallas_call | solution.py:842
  103.3 0.0 copy-done.2
  103.3 0.2 copy.7.energy_col
  103.6 0.0 copy-done.1
  103.6 0.0 copy-start
  103.6 1.0 copy-done
  104.6 1.9 %shard_map.65 = f32[4,256,256]{2,1,0:T(8,128)} custom-call(f32[2,352,128]{2,1,0:T(8,128)S(1)} %copy-done, bf16[4,256,256]{2,1,0:T(8,128)(2,1)S(1)} %copy-done.1, f32[4,256]{1,0:T(4,128)S(1)} %copy-done.2, f32[4,256,1]{2,1,0:T(8,128)S(1)} %copy.7.energy_col), custom_call_target="tpu_custom_call" | custom-call | tf_op jit(solution)/shard_map/pallas_call | solution.py:903
Async XLA Ops:
  0.0 103.3 %copy-start.2 = (f32[4,256]{1,0:T(4,128)S(1)}, f32[4,256]{1,0:T(4,128)}, u32[]{:S(2)}) copy-start(f32[4,256]{1,0:T(4,128)} %energy_row.1) | copy-start | bytes 12292
  0.0 103.6 %copy-start.1 = (bf16[4,256,256]{2,1,0:T(8,128)(2,1)S(1)}, bf16[4,256,256]{2,1,0:T(8,128)(2,1)}, u32[]{:S(2)}) copy-start(bf16[4,256,256]{2,1,0:T(8,128)(2,1)} %amp.1) | copy-start | bytes 1572868
  103.6 1.0 copy-start

commit v3 on v2

--- a/solution.py
+++ b/solution.py
@@ -1,3 +1,5 @@
+import functools
+
 import jax
 import jax.numpy as jnp
 from jax import lax
@@ -22,8 +24,16 @@
 PICKS = RING * CAP
 HALF = PICKS // 2
 DEPTH = 256
-DUO = SPLIT + 3 * REST + 8
-COUNTS = DUO - 6
+SPARE = LANES - REST
+LEFT = REST - SPARE
+FOLD_ROWS = 32
+HALF_PACK = 320
+PACK = 2 * HALF_PACK
+TOP = HALF_PACK - MAXPNO
+FOLD_AT = PACK - FOLD_ROWS - 8
+DIAG_AT = PACK - 8
+COUNTS = PACK - 4
+SQUARE_ROWS = 224
 SLOTS = 48
 SHARE = SLOTS // CORES
 HALF_SHARE = SHARE // 2
@@ -118,8 +128,12 @@
         for copy in self.gather_second():
             copy.wait_recv()
 
-    def start_delivery(self):
-        for copy in self.far() + tuple(self.near()):
+    def start_far(self):
+        for copy in self.far():
+            copy.start()
+
+    def start_near(self):
+        for copy in self.near():
             copy.start()
         self.own().start()
 
@@ -306,8 +320,12 @@
                 copies.append(self.copy(self.relay.at[way, core], dst, at + core, at + self.core, self.first_to(step, core)))
         return copies
 
-    def start_delivery(self):
-        for copy in self.far() + self.near():
+    def start_far(self):
+        for copy in self.far():
+            copy.start()
+
+    def start_near(self):
+        for copy in self.near():
             copy.start()
         self.own().start()
 
@@ -343,8 +361,8 @@
     wires, recvs = relay_bufs[0], relay_bufs[5]
     single_wires, single_recvs = single_bufs[0], single_bufs[4]
     asked, asked_smem, tables, places, request, ids, perm_main, perm_rest = scratch[34:42]
-    coeff, coeff_t, perm, blk, total, sums, fresh, same = scratch[42:50]
-    out_sems, in_sems, single_out, single_in, ask_out, ask_in, local_sems, sum_out, sum_in = scratch[50:59]
+    coeff, coeff_t, perm, blk, total, sums, fresh, same, squares = scratch[42:51]
+    out_sems, in_sems, single_out, single_in, ask_out, ask_in, local_sems, sum_out, sum_in = scratch[51:60]
     me = lax.axis_index("pairs")
     at_z = lax.axis_index("ri")
     planes = 2 * (sums.shape[1] - 1)
@@ -486,25 +504,6 @@
 
     for chunk in (2, 3):
         ports[chunk].forward_spread()
-    for chunk in (2, 3):
-        ports[chunk].finish_spread()
-    for chunk in (0, 1):
-        ports[chunk].forward_gather()
-    for chunk in (2, 3):
-        ports[chunk].start_gather()
-
-    rel_x = (owner_x + RING - at_x) & (RING - 1)
-    rel_y = (owner_y + RING - at_y) & (RING - 1)
-    place_x = ((rel_y * CORES + owner_core) * RING + rel_x) * CAP + rank - 1
-    place_y = ((rel_x * CORES + owner_core) * RING + rel_y) * CAP + rank - 1
-    tables[...] = jnp.zeros_like(tables)
-    for n, line in enumerate(lines):
-        for table, place in enumerate((order - 1, place_x, place_y)):
-            tables[table, n : n + 1, :] = jnp.sum(jnp.where(atom == line, place, 0), axis=0, keepdims=True)
-    table_copy = pltpu.make_async_copy(tables, places, local_sems.at[3])
-    table_copy.start()
-    table_copy.wait()
-
     shape = (DEPTH, DOM * BAND)
     row = lax.broadcasted_iota(jnp.int32, shape, 0)
     col = lax.broadcasted_iota(jnp.int32, shape, 1)
@@ -512,8 +511,8 @@
     late = row - split
     source = jnp.where(
         row < split,
-        (row // MAIN) * BAND + row % MAIN,
-        (late // REM) * BAND + MAIN + late % REM,
+        lax.shift_right_logical(row, 4) * BAND + (row & (MAIN - 1)),
+        lax.shift_right_arithmetic(late, 2) * BAND + MAIN + (late & (REM - 1)),
     )
     perm[...] = jnp.where((source == col) & (row < DOM * BAND), 1.0, 0.0).astype(jnp.bfloat16)
     same[...] = jnp.where(
@@ -538,11 +537,29 @@
 
         lax.fori_loop(begin // 4, end // 4, turn, 0)
 
-    half_pairs = coeff.shape[0] // 2
-    quarter = half_pairs // 2
+    prepare(0, 4)
+    for chunk in (2, 3):
+        ports[chunk].finish_spread()
+    for chunk in (0, 1):
+        ports[chunk].forward_gather()
+    for chunk in (2, 3):
+        ports[chunk].start_gather()
+
+    rel_x = (owner_x + RING - at_x) & (RING - 1)
+    rel_y = (owner_y + RING - at_y) & (RING - 1)
+    place_x = ((rel_y * CORES + owner_core) * RING + rel_x) * CAP + rank - 1
+    place_y = ((rel_x * CORES + owner_core) * RING + rel_y) * CAP + rank - 1
+    tables[...] = jnp.zeros_like(tables)
+    for n, line in enumerate(lines):
+        for table, place in enumerate((order - 1, place_x, place_y)):
+            tables[table, n : n + 1, :] = jnp.sum(jnp.where(atom == line, place, 0), axis=0, keepdims=True)
+    table_copy = pltpu.make_async_copy(tables, places, local_sems.at[3])
+    table_copy.start()
+    table_copy.wait()
+
     for single in singles:
         single.start_gather()
-    prepare(0, quarter)
+    prepare(4, 12)
 
     own_ask.wait()
     for n in range(len(peers)):
@@ -576,7 +593,14 @@
                     port.send[step, to_core, r * CAP + j] = found
             return 0
 
-        lax.fori_loop(0, RING * CORES, serve, 0)
+        lax.fori_loop(2 * CORES, 3 * CORES, serve, 0)
+        port.start_far()
+
+        def serve_near(dest, _):
+            return serve(jnp.where(dest < 2 * CORES, dest, dest + CORES), 0)
+
+        lax.fori_loop(0, 3 * CORES, serve_near, 0)
+        port.start_near()
 
     def pick(chunk):
         port = ports[chunk]
@@ -588,39 +612,46 @@
                 port.send[step, to_core, n] = port.table[asked_smem[line, CAP + chunk % 2, core * SHARE + n]]
             return 0
 
-        lax.fori_loop(0, RING * CORES, serve, 0)
+        lax.fori_loop(2 * CORES, 3 * CORES, serve, 0)
+        port.start_far()
+
+        def serve_near(dest, _):
+            return serve(jnp.where(dest < 2 * CORES, dest, dest + CORES), 0)
+
+        lax.fori_loop(0, 3 * CORES, serve_near, 0)
+        port.start_near()
 
     for chunk in (0, 1):
         ports[chunk].finish_gather()
     for chunk in (0, 1):
         ports[chunk].finish_share()
         pick(chunk)
-        ports[chunk].start_delivery()
     for chunk in (2, 3):
         ports[chunk].forward_gather()
     for single in singles:
         single.forward_gather()
-    prepare(quarter, half_pairs)
+    prepare(12, 20)
     for chunk in (0, 1):
         ports[chunk].forward_delivery()
+    prepare(20, 24)
     for chunk in (2, 3):
         ports[chunk].finish_gather()
     for n in range(2):
         singles[n].finish_gather()
         pick_single(n)
-        singles[n].start_delivery()
     for chunk in (2, 3):
         ports[chunk].finish_share()
         pick(chunk)
-        ports[chunk].start_delivery()
+    prepare(24, 32)
     for single in singles:
         single.forward_delivery()
-    prepare(half_pairs, 2 * half_pairs)
-
-    pack_row = lax.broadcasted_iota(jnp.int32, (SPLIT, LANES), 0)
-    pack_col = lax.broadcasted_iota(jnp.int32, (SPLIT, LANES), 1)
-    rest_row = lax.broadcasted_iota(jnp.int32, (REST, REST), 0)
-    rest_col = lax.broadcasted_iota(jnp.int32, (REST, REST), 1)
+    for chunk in (2, 3):
+        ports[chunk].forward_delivery()
+
+    pack_row = lax.broadcasted_iota(jnp.int32, (MAXPNO, MAXPNO), 0)
+    pack_col = lax.broadcasted_iota(jnp.int32, (MAXPNO, MAXPNO), 1)
+    pack_lane = lax.broadcasted_iota(jnp.int32, (MAXPNO, LANES), 1)
+    fold_lane = lax.broadcasted_iota(jnp.int32, (FOLD_ROWS, LANES), 1)
 
     def assemble(pair, slot, chunks):
         base = MAIN * DOM
@@ -666,132 +697,159 @@
             result += lax.dot_general(vec, vec, (((1,), (1,)), ((), ())), preferred_element_type=jnp.float32)
         return result
 
-    def first_half(step, _):
-        pair = 2 * step
-        assemble(pair + 1, 1, (0, 1))
-        total[pair] = multiply(pair, 0, early_cols)
-        assemble(jnp.minimum(pair + 2, coeff.shape[0] - 1), 0, (0, 1))
-        total[pair + 1] = multiply(pair + 1, 1, early_cols)
-        return 0
-
     early_cols = LANES * (len(RESTS[0]) + len(RESTS[1]))
     late_cols = LANES * (len(RESTS[2]) + len(RESTS[3]))
     group = coeff.shape[0] // planes
     half_ring = planes // 2
-    part = DUO // 2
-
-    def chain(way, step, duo, piece):
-        rows = pl.ds(piece * part, part)
+    part = HALF_PACK // 2
+
+    def rows_of(half, piece):
+        return pl.ds(pl.multiple_of(half * HALF_PACK + piece * part, 8), part)
+
+    def chain(way, step, half, piece):
+        rows = rows_of(half, piece)
         return pltpu.make_async_remote_copy(
-            src_ref=sums.at[way, step, duo, rows],
-            dst_ref=sums.at[way, step + 1, duo, rows],
-            send_sem=sum_out.at[(way * half_ring + step) * 2 + duo, piece],
-            recv_sem=sum_in.at[(way * half_ring + step) * 2 + duo, piece],
+            src_ref=sums.at[way, step, rows],
+            dst_ref=sums.at[way, step + 1, rows],
+            send_sem=sum_out.at[(way * half_ring + step) * 2 + half, piece],
+            recv_sem=sum_in.at[(way * half_ring + step) * 2 + half, piece],
             device_id={"ri": jnp.where(way == 0, above, below)},
             device_id_type=MESH,
         )
 
-    sends = 2 + 4 * (half_ring - 1)
-
     def locate(item):
-        later = jnp.clip(item - 2, 0, sends - 3)
-        turn = later % 4
-        opening = item < 2
-        step = jnp.where(opening, 0, 1 + later // 4)
-        way = jnp.where(opening, item, turn % 2)
-        early = jnp.logical_and(jnp.logical_not(opening), turn < 2)
-        duo = jnp.where(early, 1 - way, way)
+        step = (item + 1) // 2
+        way = jnp.where(item == 0, 0, (item + 1) % 2)
         away = jnp.where(way == 0, half_ring - step, half_ring + step)
-        mine = item >= sends
-        duo = jnp.where(mine, jnp.minimum(item - sends, 1), duo)
-        owner = jnp.where(mine, at_z, lax.rem(at_z + away, planes))
-        alone = jnp.logical_or(opening, jnp.logical_and(early, step == 1))
-        return step, way, duo, owner * group + 2 * duo, alone
-
-    def second_half(item):
-        first, following = locate(item)[3], locate(item + 1)[3]
-        assemble(first + 1, 1, (2, 3))
-        whole = [total[first] + multiply(first, 0, late_cols)]
-        assemble(following, 0, (2, 3))
-        whole.append(total[first + 1] + multiply(first + 1, 1, late_cols))
-        here, there = [w[:SPLIT, :SPLIT] for w in whole]
-        fresh[:SPLIT, :] = jnp.where(pack_row >= pack_col, here, there)
-        for n in range(2):
-            fresh[SPLIT + n * REST : SPLIT + (n + 1) * REST, :] = whole[n][SPLIT:, :SPLIT]
-        at = SPLIT + 2 * REST
-        low_here, low_there = [w[SPLIT:, SPLIT:] for w in whole]
-        fresh[at : at + REST, :REST] = jnp.where(rest_row >= rest_col, low_here, low_there)
-        at += REST
-        fresh[at : at + 1, :] = jnp.sum(jnp.where(pack_row == pack_col, there, 0.0), axis=0, keepdims=True)
-        fresh[at + 1 : at + 2, :REST] = jnp.sum(
-            jnp.where(rest_row == rest_col, low_there, 0.0), axis=0, keepdims=True
+        return way, step, lax.rem(at_z + away, planes) * group
+
+    def first_half(step, _):
+        pair = locate(step // 2)[2] + 2 * (step % 2)
+        following = locate((step + 1) // 2)[2] + 2 * ((step + 1) % 2)
+        assemble(pair + 1, 1, (0, 1))
+        total[pair] = multiply(pair, 0, early_cols)
+        assemble(following, 0, (0, 1))
+        total[pair + 1] = multiply(pair + 1, 1, early_cols)
+        return 0
+
+    def block_products(slot, first, following, whole):
+        chunks = (0, 1, 2, 3) if whole else (2, 3)
+        cols = early_cols + late_cols if whole else late_cols
+
+        def one(duo, _):
+            pair = first + 2 * duo
+            assemble(pair + 1, 1, chunks)
+            here = multiply(pair, 0, cols)
+            assemble(jnp.where(duo == 0, pair + 2, following), 0, chunks)
+            there = multiply(pair + 1, 1, cols)
+            if not whole:
+                here += total[pair]
+                there += total[pair + 1]
+            squares[duo, :MAXPNO, :MAXPNO] = jnp.where(pack_row >= pack_col, here, there)
+            diagonal = jnp.sum(jnp.where(pack_row == pack_col, there, 0.0), axis=0, keepdims=True)
+            at = DIAG_AT + 2 * duo
+            fresh[slot, pl.ds(at, 1), :] = diagonal[:, :LANES]
+            fresh[slot, pl.ds(at + 1, 1), :REST] = diagonal[:, LANES:]
+            return 0
+
+        lax.fori_loop(0, 2, one, 0)
+        fresh[slot, :MAXPNO, :] = squares[0, :MAXPNO, :LANES]
+        fresh[slot, HALF_PACK : HALF_PACK + MAXPNO, :] = squares[1, :MAXPNO, :LANES]
+        shared = jnp.where(
+            pack_lane < REST, squares[0, :MAXPNO, LANES:], pltpu.roll(squares[1, :MAXPNO, LANES:], REST, 1)
         )
-
-    def send_on(item, _):
-        step, way, duo, _, alone = locate(item)
-        second_half(item)
-
-        @pl.when(alone)
+        fresh[slot, MAXPNO:HALF_PACK, :] = shared[:TOP]
+        fresh[slot, HALF_PACK + MAXPNO : FOLD_AT, :] = shared[TOP:]
+        folded = jnp.zeros((FOLD_ROWS, LANES), jnp.float32)
+        for n in range(SQUARE_ROWS // FOLD_ROWS):
+            rows = squares[1, n * FOLD_ROWS : (n + 1) * FOLD_ROWS, LANES:]
+            moved = pltpu.roll(rows, (n * LEFT - SPARE) % LANES, 1)
+            folded = jnp.where((fold_lane >= n * LEFT) & (fold_lane < (n + 1) * LEFT), moved, folded)
+        fresh[slot, FOLD_AT:DIAG_AT, :] = folded
+
+    def begin_half(slot, way, step, half):
+        for piece in range(2):
+            rows = rows_of(half, piece)
+            sums[way, step, rows, :] = fresh[slot, rows, :]
+            chain(way, step, half, piece).start()
+
+    def add_half(way, step, half):
+        for piece in range(2):
+            rows = rows_of(half, piece)
+            chain(way, step - 1, half, piece).wait_recv()
+            sums[way, step, rows, :] = sums[way, step, rows, :] + fresh[way, rows, :]
+            chain(way, step, half, piece).start()
+
+    def ring_item(whole, item, _):
+        way, step, first = locate(item)
+        block_products(way, first, locate(item + 1)[2], whole)
+
+        @pl.when(item == 0)
         def _():
-            sums[way, step, duo] = fresh[...]
-            for piece in range(2):
-                chain(way, step, duo, piece).start()
-
-        @pl.when(jnp.logical_not(alone))
+            begin_half(0, 0, 0, 0)
+            begin_half(0, 1, 0, 1)
+
+        @pl.when(step == 1)
         def _():
-            for piece in range(2):
-                rows = slice(piece * part, (piece + 1) * part)
-                chain(way, step - 1, duo, piece).wait_recv()
-                sums[way, step, duo, rows, :] = sums[way, step, duo, rows, :] + fresh[rows, :]
-                chain(way, step, duo, piece).start()
+            begin_half(way, way, step, 1 - way)
+
+        @pl.when((step > 1) & (step < half_ring))
+        def _():
+            add_half(way, step, 1 - way)
+
+        @pl.when((way == 1) & (step < half_ring))
+        def _():
+            add_half(0, step, 0)
+            add_half(1, step, 1)
+
+        @pl.when(item == 2)
+        def _():
+            for n in range(len(peers)):
+                ask(n).wait_send()
+            for port in ports:
+                port.finish_sends()
+            for single in singles:
+                single.finish_served()
+                single.finish_sends()
 
         return 0
 
-    def send_done(item, _):
-        step, way, duo, _, _ = locate(item)
-        for piece in range(2):
-            chain(way, step, duo, piece).wait_send()
-        return 0
-
+    fresh[...] = jnp.zeros_like(fresh)
+    squares[...] = jnp.zeros_like(squares)
+    ahead = 5
     ports[0].finish_delivery()
     ports[1].finish_delivery()
-    assemble(0, 0, (0, 1))
-    lax.fori_loop(0, half_pairs // 4, first_half, 0)
-    ports[2].forward_delivery()
-    ports[3].forward_delivery()
-    lax.fori_loop(half_pairs // 4, half_pairs, first_half, 0)
+    assemble(locate(0)[2], 0, (0, 1))
+    lax.fori_loop(0, 2 * ahead, first_half, 0)
     for single in singles:
         single.finish_delivery()
     ports[2].finish_delivery()
     ports[3].finish_delivery()
-    fresh[...] = jnp.zeros_like(fresh)
-    assemble(locate(0)[3], 0, (2, 3))
-    lax.fori_loop(0, sends, send_on, 0)
-    for duo in range(2):
-        second_half(sends + duo)
+    assemble(locate(0)[2], 0, (2, 3))
+    lax.fori_loop(0, ahead, functools.partial(ring_item, False), 0)
+    assemble(locate(ahead)[2], 0, (0, 1, 2, 3))
+    lax.fori_loop(ahead, planes, functools.partial(ring_item, True), 0)
+    for half in (1, 0):
         for piece in range(2):
-            rows = slice(piece * part, (piece + 1) * part)
+            rows = rows_of(half, piece)
             for way in range(2):
-                chain(way, half_ring - 1, duo, piece).wait_recv()
-            arrived = sums[0, half_ring, duo, rows, :] + sums[1, half_ring, duo, rows, :]
-            out[duo, rows, :] = arrived + fresh[rows, :]
-        for n in range(2):
-            count = counts[at_z * group + 2 * duo + n].astype(jnp.float32)
-            out[duo, COUNTS + n : COUNTS + n + 1, :] = jnp.full((1, LANES), count)
-    lax.fori_loop(0, sends, send_done, 0)
-    for n in range(len(peers)):
-        ask(n).wait_send()
-    for port in ports:
-        port.finish_sends()
-    for single in singles:
-        single.finish_served()
-        single.finish_sends()
+                chain(way, half_ring - 1, half, piece).wait_recv()
+            arrived = sums[0, half_ring, rows, :] + sums[1, half_ring, rows, :]
+            out[rows, :] = arrived + fresh[0, rows, :]
+    for n in range(group):
+        count = counts[at_z * group + n].astype(jnp.float32)
+        out[COUNTS + n : COUNTS + n + 1, :] = jnp.full((1, LANES), count)
+    for step in range(half_ring):
+        for way in range(2):
+            for half in range(2):
+                if step or half == way:
+                    for piece in range(2):
+                        chain(way, step, half, piece).wait_send()
 
 
 def pair_products(blocks, domains, counts, coeff, planes):
     pair_dev, depth, slots = coeff.shape
     lines = 2 * RING * CORES
-    half_cols = RING * LANES * 2
     bf16 = jnp.bfloat16
     tile = (MAIN, LANES)
     scratch = []
@@ -824,11 +882,12 @@
         pltpu.VMEM((pair_dev, depth, slots), bf16),
         pltpu.VMEM((pair_dev, MAXPNO, DEPTH), bf16),
         pltpu.VMEM((DEPTH, depth), bf16),
-        pltpu.VMEM((2, DEPTH, half_cols), bf16),
+        pltpu.VMEM((2, DEPTH, blocks.shape[2]), bf16),
         pltpu.VMEM((pair_dev, MAXPNO, MAXPNO), jnp.float32),
-        pltpu.VMEM((2, planes // 2 + 1, 2, DUO, LANES), jnp.float32),
-        pltpu.VMEM((DUO, LANES), jnp.float32),
+        pltpu.VMEM((2, planes // 2 + 1, PACK, LANES), jnp.float32),
+        pltpu.VMEM((2, PACK, LANES), jnp.float32),
         pltpu.VMEM((MAXPNO, slots), bf16),
+        pltpu.VMEM((2, SQUARE_ROWS, 2 * LANES), jnp.float32),
         pltpu.SemaphoreType.DMA((4, 27)),
         pltpu.SemaphoreType.DMA((4, 27)),
         pltpu.SemaphoreType.DMA((2, 16)),
@@ -841,7 +900,7 @@
     ]
     return pl.pallas_call(
         main_kernel,
-        out_shape=jax.ShapeDtypeStruct((2, DUO, LANES), jnp.float32),
+        out_shape=jax.ShapeDtypeStruct((PACK, LANES), jnp.float32),
         in_specs=[
             pl.BlockSpec(memory_space=pltpu.VMEM),
             pl.BlockSpec(memory_space=pltpu.VMEM),
@@ -857,31 +916,48 @@
 def tail_kernel(packed, amp, energy_row, energy_col, out, wide):
     slots = amp.shape[1]
     step = pl.program_id(0)
-    row = lax.broadcasted_iota(jnp.int32, (SPLIT, LANES), 0)
-    col = lax.broadcasted_iota(jnp.int32, (SPLIT, LANES), 1)
-    low_row, low_col = row[:REST], col[:REST]
     full_row = lax.broadcasted_iota(jnp.int32, (slots, slots), 0)
     full_col = lax.broadcasted_iota(jnp.int32, (slots, slots), 1)
+    lane = lax.broadcasted_iota(jnp.int32, (MAXPNO, LANES), 1)
+    fold_lane = lax.broadcasted_iota(jnp.int32, (FOLD_ROWS, LANES), 1)
+    wide[MAXPNO:, :] = jnp.zeros((slots - MAXPNO, slots), jnp.float32)
+
+    def shared_at(begin, end):
+        if end <= TOP:
+            return packed[MAXPNO + begin : MAXPNO + end, :]
+        return packed[HALF_PACK + MAXPNO + begin - TOP : HALF_PACK + MAXPNO + end - TOP, :]
+
+    @pl.when(step == 0)
+    def _():
+        wide[:MAXPNO, :LANES] = packed[:MAXPNO, :]
+        for begin, end in ((0, TOP), (TOP, MAXPNO)):
+            wide[begin:end, LANES:] = jnp.where(lane[begin:end] < REST, shared_at(begin, end), 0.0)
+
+    @pl.when(step == 1)
+    def _():
+        wide[:MAXPNO, :LANES] = packed[HALF_PACK : HALF_PACK + MAXPNO, :]
+        for begin, end in ((0, TOP), (TOP, MAXPNO)):
+            turned = pltpu.roll(shared_at(begin, end), SPARE, 1)
+            wide[begin:end, LANES:] = jnp.where(lane[begin:end] < SPARE, turned, 0.0)
+        folded = packed[FOLD_AT:DIAG_AT, :]
+        for n in range(SQUARE_ROWS // FOLD_ROWS):
+            begin, end = n * FOLD_ROWS, min((n + 1) * FOLD_ROWS, MAXPNO)
+            moved = pltpu.roll(folded, (SPARE - n * LEFT) % LANES, 1)
+            left = (fold_lane >= SPARE) & (fold_lane < REST)
+            held = wide[begin:end, LANES:]
+            wide[begin:end, LANES:] = jnp.where(left[: end - begin], moved[: end - begin], held)
+
+    square = wide[...]
+    at = DIAG_AT + 2 * step
+    diagonal = jnp.concatenate([packed[pl.ds(at, 1), :], packed[pl.ds(at + 1, 1), :]], axis=1)
+    on_diagonal = full_row == full_col
     for n in range(2):
-        first = packed[0, :SPLIT, :]
-        rest = packed[0, SPLIT + 2 * REST : SPLIT + 3 * REST, :]
+        count = packed[pl.ds(COUNTS + 2 * step + n, 1), :][:, :1].astype(jnp.int32)
         if n == 0:
-            first = jnp.where(row >= col, first, 0.0)
-            rest = jnp.where(low_row >= low_col, rest, 0.0)
+            held = jnp.where(full_row >= full_col, square, 0.0)
         else:
-            at = SPLIT + 3 * REST
-            first = jnp.where(row < col, first, jnp.where(row == col, packed[0, at : at + 1, :], 0.0))
-            rest = jnp.where((low_row < low_col) & (low_col < REST), rest, 0.0)
-            rest = jnp.where(low_row == low_col, packed[0, at + 1 : at + 2, :], rest)
-        wide[n, :SPLIT, :LANES] = first
-        wide[n, :SPLIT, LANES:] = jnp.zeros((SPLIT, slots - LANES), jnp.float32)
-        wide[n, SPLIT : SPLIT + REST, :LANES] = packed[0, SPLIT + n * REST : SPLIT + (n + 1) * REST, :]
-        wide[n, SPLIT : SPLIT + REST, LANES:] = rest
-        wide[n, MAXPNO:, :] = jnp.zeros((slots - MAXPNO, slots), jnp.float32)
-    for n in range(2):
-        count = packed[0, COUNTS + n : COUNTS + n + 1, :1].astype(jnp.int32)
-        held = wide[n]
-        products = held + jnp.where(full_row == full_col, 0.0, held.T)
+            held = jnp.where(full_row < full_col, square, jnp.where(on_diagonal, diagonal, 0.0))
+        products = held + jnp.where(on_diagonal, 0.0, held.T)
         valid = (full_row < count) & (full_col < count)
         products = jnp.where(valid, products / NAUX, 0.0)
         amps = amp[n]
@@ -905,13 +981,13 @@
         out_shape=jax.ShapeDtypeStruct((subs, slots, slots), jnp.float32),
         grid=(subs // 2,),
         in_specs=[
-            pl.BlockSpec((1, DUO, LANES), lambda i: (i, 0, 0)),
+            pl.BlockSpec((PACK, LANES), lambda i: (0, 0)),
             pl.BlockSpec((2, slots, slots), lambda i: (i, 0, 0)),
             pl.BlockSpec((subs, slots), lambda i: (0, 0)),
             pl.BlockSpec((2, slots, 1), lambda i: (i, 0, 0)),
         ],
         out_specs=pl.BlockSpec((2, slots, slots), lambda i: (i, 0, 0)),
-        scratch_shapes=[pltpu.VMEM((2, slots, slots), jnp.float32)],
+        scratch_shapes=[pltpu.VMEM((slots, slots), jnp.float32)],
         compiler_params=params(32),
     )(packed, amp, energy, energy[:, :, None])
 

time: 107 us -> 101 us (0.944); the launches traced: 106 us -> 99.3 us
  Pallas kernels: 105 us -> 98.1 us
    pallas_call x1, Pallas kernels: 103 us -> 96.1 us  [pair_products(): pl.pallas_call(main_kernel, out_shape=jax.ShapeDtypeStruct((PACK, LANES),...]
where the time goes in v3:
time: 101 us; the launch traced here: 99.3 us
  Pallas kernels  98.1 us (97%)
  local copies, waits for them, and re-layouts  1.19 us (1%)
    pallas_call x1, Pallas kernels, pair_products(): pl.pallas_call(main_kernel, out_shape=jax.ShapeDtypeStruct((PACK, LANES),...  96.1 us
    pallas_call x1, Pallas kernels, tail(): pl.pallas_call(tail_kernel, out_shape=jax.ShapeDtypeStruct((subs, slots,...  2.05 us

profile of v3, /device:TPU:1, one launch (start us, length us, event | category | flops | bytes accessed | tf_op | source)
XLA Modules:
  0.0 99.3 jit_solution(2181324307663157783)
XLA Ops:
  0.0 0.0 copy-start.2
  0.0 0.0 copy-start.1
  0.0 96.1 %shard_map.64.packed = f32[640,128]{1,0:T(8,128)} custom-call(bf16[20,16,1792]{2,1,0:T(8,128)(2,1)} %bitcast.4, s32[12,32]{1,0:T(8,128)} %bitcast.5, s32[32]{0:T(128)} %counts.1, bf16[32,240,256]{2,1,0:T(8,128)(2,1)} %coeff_hbm.1), custom_call_target="tpu_custom_call" | custom-call | tf_op jit(solution)/shard_map/pallas_call | solution.py:901
  96.1 0.0 copy-done.2
  96.1 0.2 copy.7.energy_col
  96.3 0.0 copy-done.1
  96.3 0.0 copy-start
  96.3 1.0 copy-done
  97.3 2.0 %shard_map.65 = f32[4,256,256]{2,1,0:T(8,128)} custom-call(f32[640,128]{1,0:T(8,128)S(1)} %copy-done, bf16[4,256,256]{2,1,0:T(8,128)(2,1)S(1)} %copy-done.1, f32[4,256]{1,0:T(4,128)S(1)} %copy-done.2, f32[4,256,1]{2,1,0:T(8,128)S(1)} %copy.7.energy_col), custom_call_target="tpu_custom_call" | custom-call | tf_op jit(solution)/shard_map/pallas_call | solution.py:979
Async XLA Ops:
  0.0 96.1 %copy-start.2 = (f32[4,256]{1,0:T(4,128)S(1)}, f32[4,256]{1,0:T(4,128)}, u32[]{:S(2)}) copy-start(f32[4,256]{1,0:T(4,128)} %energy_row.1) | copy-start | bytes 12292
  0.0 96.3 %copy-start.1 = (bf16[4,256,256]{2,1,0:T(8,128)(2,1)S(1)}, bf16[4,256,256]{2,1,0:T(8,128)(2,1)}, u32[]{:S(2)}) copy-start(bf16[4,256,256]{2,1,0:T(8,128)(2,1)} %amp.1) | copy-start | bytes 1572868
  96.3 1.0 copy-start

commit v4 on v3

--- a/solution.py
+++ b/solution.py
@@ -456,54 +456,73 @@
         ports[chunk].finish_spread()
         ports[chunk].start_gather()
 
-    ids[...] = jnp.zeros_like(ids)
+    for chunk in (2, 3):
+        ports[chunk].forward_spread()
+
+    def parts_of(atom):
+        owner = lax.shift_right_logical(atom, 4)
+        chip = lax.shift_right_logical(owner, 1)
+        return owner, owner & (CORES - 1), chip & (RING - 1), lax.shift_right_logical(chip, 2), atom & (ATOMS - 1)
+
+    map_shape = (8, LANES)
+    map_row = lax.broadcasted_iota(jnp.int32, map_shape, 0)
+    map_lane = lax.broadcasted_iota(jnp.int32, map_shape, 1)
+    atom_map = map_row * LANES + map_lane
     pairs = domains.shape[1]
-    fold = LANES // pairs
-    ids[: domains.shape[0], :pairs] = domains[...]
-    held = ids[...]
-    lane = lax.broadcasted_iota(jnp.int32, held.shape, 1)
-    turned = [held if n == 0 else pltpu.roll(held, n * pairs, 1) for n in range(fold)]
-    lines = []
-    for line in range(DOM // fold):
-        row = jnp.zeros((1, LANES), jnp.int32)
-        for n in range(fold):
-            k = line * fold + n
-            row = jnp.where(lane[:1] // pairs == n, turned[n][k : k + 1], row)
-        lines.append(row)
-    flat_shape = (ATOMS * RING * RING * CORES, LANES)
-    atom = lax.broadcasted_iota(jnp.int32, flat_shape, 0)
-    lane_at = lax.broadcasted_iota(jnp.int32, flat_shape, 1)
-    named = jnp.zeros(flat_shape, jnp.int32)
-    for line in lines:
-        named = jnp.where(atom == line, 1, named)
-    named = jnp.broadcast_to(jnp.max(named, axis=1, keepdims=True), flat_shape)
-    local = atom & (ATOMS - 1)
-    owner = lax.shift_right_logical(atom, 4)
+
+    def mark(pair, seen):
+        for k in range(DOM):
+            seen = jnp.where(atom_map == domains[k, pair], 1, seen)
+        return seen
+
+    named = lax.fori_loop(0, pairs, mark, jnp.zeros(map_shape, jnp.int32))
+    owner, owner_core, owner_x, owner_y, local = parts_of(atom_map)
     rank = named
     for shift in (1, 2, 4, 8):
-        rank = rank + jnp.where(local >= shift, pltpu.roll(rank, shift, 0), 0)
+        rank = rank + jnp.where(local >= shift, pltpu.roll(rank, shift, 1), 0)
     order = named
-    for shift in (1, 2, 4, 8, 16, 32, 64, 128, 256):
-        order = order + jnp.where(atom >= shift, pltpu.roll(order, shift, 0), 0)
-    own_lane = jnp.where((owner == lane_at) & (named > 0), local, 0)
-    for j in range(CAP):
-        request[j : j + 1, :] = jnp.sum(jnp.where(rank == j + 1, own_lane, 0), axis=0, keepdims=True)
-    owner_chip = lax.shift_right_logical(owner, 1)
-    owner_core = owner & (CORES - 1)
-    owner_x, owner_y = owner_chip & (RING - 1), lax.shift_right_logical(owner_chip, 2)
-    taken = (order == lane_at + 1) & (named > 0)
-    for n, (u, v) in enumerate(((owner_x, owner_y), (owner_y, owner_x))):
-        held_at = ((v * CORES + owner_core) * RING + u) * ATOMS + local
-        request[CAP + n : CAP + n + 1, :] = jnp.sum(jnp.where(taken, held_at, 0), axis=0, keepdims=True)
+    for shift in (1, 2, 4, 8, 16, 32, 64):
+        order = order + jnp.where(map_lane >= shift, pltpu.roll(order, shift, 1), 0)
+    counted = order
+    map_rows = ATOMS * RING * RING * CORES // LANES
+    for n in range(map_rows - 1):
+        order = order + jnp.where(map_row > n, counted[n : n + 1, LANES - 1 :], 0)
+    rel_x = (owner_x + RING - at_x) & (RING - 1)
+    rel_y = (owner_y + RING - at_y) & (RING - 1)
+    tables[0] = order - 1
+    tables[1] = ((rel_y * CORES + owner_core) * RING + rel_x) * CAP + rank - 1
+    tables[2] = ((rel_x * CORES + owner_core) * RING + rel_y) * CAP + rank - 1
+    table_copy = pltpu.make_async_copy(tables, places, local_sems.at[3])
+    table_copy.start()
+
+    ids[:map_rows, :] = jnp.where(named > 0, order, 0)[:map_rows]
+    ids[map_rows:, :] = jnp.where(named > 0, rank, 0)[:map_rows]
+    upright = ids[...].T
+    list_shape = (LANES, LANES)
+    list_row = lax.broadcasted_iota(jnp.int32, list_shape, 0)
+    list_lane = lax.broadcasted_iota(jnp.int32, list_shape, 1)
+    rows = [jnp.zeros((1, LANES), jnp.int32) for _ in range(CAP + 2)]
+    for n in range(map_rows):
+        owner, owner_core, owner_x, owner_y, local = parts_of(list_row + n * LANES)
+        own_lane = jnp.where(owner == list_lane, local, 0)
+        order_at = jnp.broadcast_to(upright[:, n : n + 1], list_shape)
+        rank_at = jnp.broadcast_to(upright[:, map_rows + n : map_rows + n + 1], list_shape)
+        for j in range(CAP):
+            rows[j] += jnp.sum(jnp.where(rank_at == j + 1, own_lane, 0), axis=0, keepdims=True)
+        for j, (u, v) in enumerate(((owner_x, owner_y), (owner_y, owner_x))):
+            held_at = ((v * CORES + owner_core) * RING + u) * ATOMS + local
+            rows[CAP + j] += jnp.sum(jnp.where(order_at == list_lane + 1, held_at, 0), axis=0, keepdims=True)
+    for n in range(CAP + 2):
+        request[n : n + 1, :] = rows[n]
     request[CAP + 2 :, :] = jnp.zeros((6 - CAP, LANES), jnp.int32)
 
     for n in range(len(peers)):
         ask(n).start()
     own_ask = pltpu.make_async_copy(request, asked.at[core], local_sems.at[1])
     own_ask.start()
-
     for chunk in (2, 3):
-        ports[chunk].forward_spread()
+        ports[chunk].finish_spread()
+
     shape = (DEPTH, DOM * BAND)
     row = lax.broadcasted_iota(jnp.int32, shape, 0)
     col = lax.broadcasted_iota(jnp.int32, shape, 1)
@@ -538,24 +557,10 @@
         lax.fori_loop(begin // 4, end // 4, turn, 0)
 
     prepare(0, 4)
-    for chunk in (2, 3):
-        ports[chunk].finish_spread()
     for chunk in (0, 1):
         ports[chunk].forward_gather()
     for chunk in (2, 3):
         ports[chunk].start_gather()
-
-    rel_x = (owner_x + RING - at_x) & (RING - 1)
-    rel_y = (owner_y + RING - at_y) & (RING - 1)
-    place_x = ((rel_y * CORES + owner_core) * RING + rel_x) * CAP + rank - 1
-    place_y = ((rel_x * CORES + owner_core) * RING + rel_y) * CAP + rank - 1
-    tables[...] = jnp.zeros_like(tables)
-    for n, line in enumerate(lines):
-        for table, place in enumerate((order - 1, place_x, place_y)):
-            tables[table, n : n + 1, :] = jnp.sum(jnp.where(atom == line, place, 0), axis=0, keepdims=True)
-    table_copy = pltpu.make_async_copy(tables, places, local_sems.at[3])
-    table_copy.start()
-    table_copy.wait()
 
     for single in singles:
         single.start_gather()
@@ -658,8 +663,10 @@
         begin = 0
         upper = lax.broadcasted_iota(jnp.int32, (8, LANES), 0) < REM
 
+        names = [domains[k, pair] for k in range(DOM)]
+
         def named_at(table):
-            return [places[table, k // fold, (k % fold) * pairs + pair] for k in range(DOM)]
+            return [places[table, lax.shift_right_logical(a, 7), a & (LANES - 1)] for a in names]
 
         at = named_at(0)
         for chunk in chunks:
@@ -816,7 +823,8 @@
 
     fresh[...] = jnp.zeros_like(fresh)
     squares[...] = jnp.zeros_like(squares)
-    ahead = 5
+    ahead = 4
+    table_copy.wait()
     ports[0].finish_delivery()
     ports[1].finish_delivery()
     assemble(locate(0)[2], 0, (0, 1))
@@ -876,7 +884,7 @@
         pltpu.VMEM((3, 8, LANES), jnp.int32),
         pltpu.SMEM((3, 8, LANES), jnp.int32),
         pltpu.VMEM((8, LANES), jnp.int32),
-        pltpu.VMEM((16, LANES), jnp.int32),
+        pltpu.VMEM((8, LANES), jnp.int32),
         pltpu.VMEM((ATOMS * MAIN, ATOMS * MAIN), bf16),
         pltpu.VMEM((ATOMS * MAIN, ATOMS * MAIN), bf16),
         pltpu.VMEM((pair_dev, depth, slots), bf16),
@@ -900,10 +908,10 @@
     ]
     return pl.pallas_call(
         main_kernel,
-        out_shape=jax.ShapeDtypeStruct((PACK, LANES), jnp.float32),
+        out_shape=pltpu.VMEM((PACK, LANES), jnp.float32),
         in_specs=[
             pl.BlockSpec(memory_space=pltpu.VMEM),
-            pl.BlockSpec(memory_space=pltpu.VMEM),
+            pl.BlockSpec(memory_space=pltpu.SMEM),
             pl.BlockSpec(memory_space=pltpu.SMEM),
             pl.BlockSpec(memory_space=pl.ANY),
         ],

time: 101 us -> 98.2 us (0.972); the launches traced: 99.3 us -> 98.1 us
  no operation moved by 1% of the time
where the time goes in v4:
time: 98.2 us; the launch traced here: 98.1 us
  Pallas kernels  97.8 us (100%)
    pallas_call x1, Pallas kernels, pair_products(): pl.pallas_call(main_kernel, out_shape=pltpu.VMEM((PACK, LANES), jnp.float...  95.7 us
    pallas_call x1, Pallas kernels, tail(): pl.pallas_call(tail_kernel, out_shape=jax.ShapeDtypeStruct((subs, slots,...  2.08 us

profile of v4, /device:TPU:1, one launch (start us, length us, event | category | flops | bytes accessed | tf_op | source)
XLA Modules:
  0.0 98.1 jit_solution(18166945510730902842)
XLA Ops:
  0.0 0.0 copy-start.1
  0.0 0.0 copy-start
  0.0 95.7 %shard_map.64.packed = f32[640,128]{1,0:T(8,128)S(1)} custom-call(bf16[20,16,1792]{2,1,0:T(8,128)(2,1)} %bitcast.4, s32[12,32]{1,0:T(8,128)} %bitcast.5, s32[32]{0:T(128)} %counts.1, bf16[32,240,256]{2,1,0:T(8,128)(2,1)} %coeff_hbm.1), custom_call_target="tpu_custom_call" | custom-call | tf_op jit(solution)/shard_map/pallas_call | solution.py:909
  95.7 0.0 copy-done.1
  95.7 0.2 copy.7.energy_col
  96.0 0.0 copy-done
  96.0 2.1 %shard_map.65 = f32[4,256,256]{2,1,0:T(8,128)} custom-call(f32[640,128]{1,0:T(8,128)S(1)} %shard_map.64.packed, bf16[4,256,256]{2,1,0:T(8,128)(2,1)S(1)} %copy-done, f32[4,256]{1,0:T(4,128)S(1)} %copy-done.1, f32[4,256,1]{2,1,0:T(8,128)S(1)} %copy.7.energy_col), custom_call_target="tpu_custom_call" | custom-call | tf_op jit(solution)/shard_map/pallas_call | solution.py:987
Async XLA Ops:
  0.0 95.7 %copy-start.1 = (f32[4,256]{1,0:T(4,128)S(1)}, f32[4,256]{1,0:T(4,128)}, u32[]{:S(2)}) copy-start(f32[4,256]{1,0:T(4,128)} %energy_row.1) | copy-start | bytes 12292
  0.0 96.0 %copy-start = (bf16[4,256,256]{2,1,0:T(8,128)(2,1)S(1)}, bf16[4,256,256]{2,1,0:T(8,128)(2,1)}, u32[]{:S(2)}) copy-start(bf16[4,256,256]{2,1,0:T(8,128)(2,1)} %amp.1) | copy-start | bytes 1572868

commit v5 on v4

--- a/solution.py
+++ b/solution.py
@@ -354,15 +354,15 @@
 
 
 def main_kernel(
-    blocks, domains, counts, coeff_hbm, out, *scratch
+    blocks_hbm, domains, counts, coeff_hbm, out, *scratch
 ):
     relay_bufs = [scratch[4 * n : 4 * n + 4] for n in range(6)]
     single_bufs = [scratch[24 + 2 * n : 26 + 2 * n] for n in range(5)]
     wires, recvs = relay_bufs[0], relay_bufs[5]
     single_wires, single_recvs = single_bufs[0], single_bufs[4]
     asked, asked_smem, tables, places, request, ids, perm_main, perm_rest = scratch[34:42]
-    coeff, coeff_t, perm, blk, total, sums, fresh, same, squares = scratch[42:51]
-    out_sems, in_sems, single_out, single_in, ask_out, ask_in, local_sems, sum_out, sum_in = scratch[51:60]
+    coeff, coeff_t, perm, blk, total, sums, fresh, same, squares, blocks = scratch[42:52]
+    out_sems, in_sems, single_out, single_in, ask_out, ask_in, local_sems, sum_out, sum_in = scratch[52:61]
     me = lax.axis_index("pairs")
     at_z = lax.axis_index("ri")
     planes = 2 * (sums.shape[1] - 1)
@@ -387,8 +387,6 @@
             )
     peers.append((along_x(0, 1 - core), 1 - core, core))
 
-    fetch = pltpu.make_async_copy(coeff_hbm, coeff, local_sems.at[0])
-    fetch.start()
     barrier = pltpu.get_barrier_semaphore()
     for peer, _, _ in peers:
         pl.semaphore_signal(barrier, inc=1, device_id={"pairs": peer}, device_id_type=MESH)
@@ -419,6 +417,17 @@
         bufs = [group_bufs[n] for group_bufs in single_bufs]
         singles.append(Ports(n, gather_to, deliver_to, *bufs, single_out, single_in, core))
 
+    fetches = []
+    for chunk in range(4):
+        tiles = RESTS[chunk]
+        cols = pl.ds(tiles[0] * LANES, len(tiles) * LANES)
+        fetches.append(
+            pltpu.make_async_copy(blocks_hbm.at[:, :, cols], blocks.at[:, :, cols], local_sems.at[4 + chunk])
+        )
+        fetches[chunk].start()
+    fetch = pltpu.make_async_copy(coeff_hbm, coeff, local_sems.at[0])
+    fetch.start()
+
     square = (ATOMS * MAIN, ATOMS * MAIN)
     out_at = lax.broadcasted_iota(jnp.int32, square, 0)
     from_at = lax.broadcasted_iota(jnp.int32, square, 1)
@@ -433,6 +442,7 @@
         return jnp.dot(perm_main[...], flat, preferred_element_type=jnp.float32).astype(jnp.bfloat16)
 
     def form(chunk):
+        fetches[chunk].wait()
         main = main_rows(MAINS[chunk])
         for n in range(len(MAINS[chunk])):
             wires[chunk][n] = main[:, n * LANES : (n + 1) * LANES].reshape(ATOMS, MAIN, LANES)
@@ -697,12 +707,12 @@
 
     def multiply(pair, slot, cols):
         weights = coeff_t[pair]
-        result = jnp.zeros((MAXPNO, MAXPNO), jnp.float32)
+        vecs = []
         for at in range(0, cols, 256):
             vec = jnp.dot(weights, blk[slot, :, at : at + 256], preferred_element_type=jnp.float32)
-            vec = vec.astype(jnp.bfloat16)
-            result += lax.dot_general(vec, vec, (((1,), (1,)), ((), ())), preferred_element_type=jnp.float32)
-        return result
+            vecs.append(vec.astype(jnp.bfloat16))
+        vecs = jnp.concatenate(vecs, axis=1)
+        return lax.dot_general(vecs, vecs, (((1,), (1,)), ((), ())), preferred_element_type=jnp.float32)
 
     early_cols = LANES * (len(RESTS[0]) + len(RESTS[1]))
     late_cols = LANES * (len(RESTS[2]) + len(RESTS[3]))
@@ -896,13 +906,14 @@
         pltpu.VMEM((2, PACK, LANES), jnp.float32),
         pltpu.VMEM((MAXPNO, slots), bf16),
         pltpu.VMEM((2, SQUARE_ROWS, 2 * LANES), jnp.float32),
+        pltpu.VMEM(blocks.shape, bf16),
         pltpu.SemaphoreType.DMA((4, 27)),
         pltpu.SemaphoreType.DMA((4, 27)),
         pltpu.SemaphoreType.DMA((2, 16)),
         pltpu.SemaphoreType.DMA((2, 16)),
         pltpu.SemaphoreType.DMA((lines,)),
         pltpu.SemaphoreType.DMA((lines,)),
-        pltpu.SemaphoreType.DMA((4,)),
+        pltpu.SemaphoreType.DMA((8,)),
         pltpu.SemaphoreType.DMA((2 * planes, 2)),
         pltpu.SemaphoreType.DMA((2 * planes, 2)),
     ]
@@ -910,7 +921,7 @@
         main_kernel,
         out_shape=pltpu.VMEM((PACK, LANES), jnp.float32),
         in_specs=[
-            pl.BlockSpec(memory_space=pltpu.VMEM),
+            pl.BlockSpec(memory_space=pl.ANY),
             pl.BlockSpec(memory_space=pltpu.SMEM),
             pl.BlockSpec(memory_space=pltpu.SMEM),
             pl.BlockSpec(memory_space=pl.ANY),

time: 98.2 us -> 97 us (0.988)
  Pallas kernels: 97.8 us -> 96.6 us
    pallas_call x1, Pallas kernels: 95.7 us -> 94.6 us  [pair_products(): pl.pallas_call(main_kernel, out_shape=pltpu.VMEM((PACK, LANES), jnp.float...]
where the time goes in v5:
time: 97 us; the launch traced here: 96.9 us
  Pallas kernels  96.6 us (100%)
    pallas_call x1, Pallas kernels, pair_products(): pl.pallas_call(main_kernel, out_shape=pltpu.VMEM((PACK, LANES), jnp.float...  94.6 us
    pallas_call x1, Pallas kernels, tail(): pl.pallas_call(tail_kernel, out_shape=jax.ShapeDtypeStruct((subs, slots,...  2.08 us

profile of v5, /device:TPU:1, one launch (start us, length us, event | category | flops | bytes accessed | tf_op | source)
XLA Modules:
  0.0 96.9 jit_solution(16938807598901412485)
XLA Ops:
  0.0 0.0 copy-start.1
  0.0 0.0 copy-start
  0.0 94.6 %shard_map.64.packed = f32[640,128]{1,0:T(8,128)S(1)} custom-call(bf16[20,16,1792]{2,1,0:T(8,128)(2,1)} %bitcast.4, s32[12,32]{1,0:T(8,128)} %bitcast.5, s32[32]{0:T(128)} %counts.1, bf16[32,240,256]{2,1,0:T(8,128)(2,1)} %coeff_hbm.1), custom_call_target="tpu_custom_call" | custom-call | tf_op jit(solution)/shard_map/pallas_call | solution.py:920
  94.6 0.0 copy-done.1
  94.6 0.2 copy.7.energy_col
  94.8 0.0 copy-done
  94.8 2.1 %shard_map.65 = f32[4,256,256]{2,1,0:T(8,128)} custom-call(f32[640,128]{1,0:T(8,128)S(1)} %shard_map.64.packed, bf16[4,256,256]{2,1,0:T(8,128)(2,1)S(1)} %copy-done, f32[4,256]{1,0:T(4,128)S(1)} %copy-done.1, f32[4,256,1]{2,1,0:T(8,128)S(1)} %copy.7.energy_col), custom_call_target="tpu_custom_call" | custom-call | tf_op jit(solution)/shard_map/pallas_call | solution.py:998
Async XLA Ops:
  0.0 94.6 %copy-start.1 = (f32[4,256]{1,0:T(4,128)S(1)}, f32[4,256]{1,0:T(4,128)}, u32[]{:S(2)}) copy-start(f32[4,256]{1,0:T(4,128)} %energy_row.1) | copy-start | bytes 12292
  0.0 94.8 %copy-start = (bf16[4,256,256]{2,1,0:T(8,128)(2,1)S(1)}, bf16[4,256,256]{2,1,0:T(8,128)(2,1)}, u32[]{:S(2)}) copy-start(bf16[4,256,256]{2,1,0:T(8,128)(2,1)} %amp.1) | copy-start | bytes 1572868

commit v6 on v5

--- a/solution.py
+++ b/solution.py
@@ -551,30 +551,40 @@
         blk[n, DOM * BAND :, :] = jnp.zeros((DEPTH - DOM * BAND, blk.shape[2]), jnp.bfloat16)
     fetch.wait()
 
+    group = coeff.shape[0] // planes
+    half_ring = planes // 2
+
+    def locate(item):
+        step = (item + 1) // 2
+        way = jnp.where(item == 0, 0, (item + 1) % 2)
+        away = jnp.where(way == 0, half_ring - step, half_ring + step)
+        return way, step, lax.rem(at_z + away, planes) * group
+
     def prepare(begin, end):
-        def turn(pair, _):
+        def turn(item, _):
+            first = locate(item)[2]
             ordered = [
-                jnp.dot(perm[...], coeff[4 * pair + n], preferred_element_type=jnp.float32).astype(jnp.bfloat16)
-                for n in range(4)
+                jnp.dot(perm[...], coeff[first + n], preferred_element_type=jnp.float32).astype(jnp.bfloat16)
+                for n in range(group)
             ]
-            for n in range(4):
+            for n in range(group):
                 turned = lax.dot_general(
                     same[...], ordered[n], (((1,), (1,)), ((), ())), preferred_element_type=jnp.float32
                 )
-                coeff_t[4 * pair + n] = turned.astype(jnp.bfloat16)
+                coeff_t[first + n] = turned.astype(jnp.bfloat16)
             return 0
 
-        lax.fori_loop(begin // 4, end // 4, turn, 0)
-
-    prepare(0, 4)
+        lax.fori_loop(begin, end, turn, 0)
+
+    prepare(0, 1)
+    for chunk in (2, 3):
+        ports[chunk].start_gather()
     for chunk in (0, 1):
         ports[chunk].forward_gather()
-    for chunk in (2, 3):
-        ports[chunk].start_gather()
 
     for single in singles:
         single.start_gather()
-    prepare(4, 12)
+    prepare(1, 3)
 
     own_ask.wait()
     for n in range(len(peers)):
@@ -645,10 +655,10 @@
         ports[chunk].forward_gather()
     for single in singles:
         single.forward_gather()
-    prepare(12, 20)
+    prepare(3, 5)
     for chunk in (0, 1):
         ports[chunk].forward_delivery()
-    prepare(20, 24)
+    prepare(5, 6)
     for chunk in (2, 3):
         ports[chunk].finish_gather()
     for n in range(2):
@@ -657,7 +667,7 @@
     for chunk in (2, 3):
         ports[chunk].finish_share()
         pick(chunk)
-    prepare(24, 32)
+    prepare(6, planes - 1)
     for single in singles:
         single.forward_delivery()
     for chunk in (2, 3):
@@ -716,8 +726,6 @@
 
     early_cols = LANES * (len(RESTS[0]) + len(RESTS[1]))
     late_cols = LANES * (len(RESTS[2]) + len(RESTS[3]))
-    group = coeff.shape[0] // planes
-    half_ring = planes // 2
     part = HALF_PACK // 2
 
     def rows_of(half, piece):
@@ -733,12 +741,6 @@
             device_id={"ri": jnp.where(way == 0, above, below)},
             device_id_type=MESH,
         )
-
-    def locate(item):
-        step = (item + 1) // 2
-        way = jnp.where(item == 0, 0, (item + 1) % 2)
-        away = jnp.where(way == 0, half_ring - step, half_ring + step)
-        return way, step, lax.rem(at_z + away, planes) * group
 
     def first_half(step, _):
         pair = locate(step // 2)[2] + 2 * (step % 2)
@@ -799,6 +801,11 @@
 
     def ring_item(whole, item, _):
         way, step, first = locate(item)
+
+        @pl.when(item == planes - 1)
+        def _():
+            prepare(planes - 1, planes)
+
         block_products(way, first, locate(item + 1)[2], whole)
 
         @pl.when(item == 0)
@@ -833,7 +840,7 @@
 
     fresh[...] = jnp.zeros_like(fresh)
     squares[...] = jnp.zeros_like(squares)
-    ahead = 4
+    ahead = 3
     table_copy.wait()
     ports[0].finish_delivery()
     ports[1].finish_delivery()
@@ -972,12 +979,13 @@
     on_diagonal = full_row == full_col
     for n in range(2):
         count = packed[pl.ds(COUNTS + 2 * step + n, 1), :][:, :1].astype(jnp.int32)
+        row, col = full_row[:MAXPNO], full_col[:MAXPNO]
         if n == 0:
             held = jnp.where(full_row >= full_col, square, 0.0)
         else:
             held = jnp.where(full_row < full_col, square, jnp.where(on_diagonal, diagonal, 0.0))
-        products = held + jnp.where(on_diagonal, 0.0, held.T)
-        valid = (full_row < count) & (full_col < count)
+        products = held[:MAXPNO] + jnp.where(row == col, 0.0, held.T[:MAXPNO])
+        valid = (row < count) & (col < count)
         products = jnp.where(valid, products / NAUX, 0.0)
         amps = amp[n]
         contract = (((1,), (1,)), ((), ()))
@@ -988,9 +996,10 @@
         coupled = lax.dot_general(low, amps, contract, preferred_element_type=jnp.float32)
         coupled += lax.dot_general(mid, amps, contract, preferred_element_type=jnp.float32)
         coupled += lax.dot_general(high, amps, contract, preferred_element_type=jnp.float32)
-        energies = energy_col[n] + energy_row[pl.ds(2 * step + n, 1), :]
-        result = products + coupled + energies * amps.astype(jnp.float32)
-        out[n] = jnp.where(valid, result, 0.0)
+        energies = energy_col[n, :MAXPNO] + energy_row[pl.ds(2 * step + n, 1), :]
+        result = products + coupled + energies * amps[:MAXPNO].astype(jnp.float32)
+        out[n, :MAXPNO] = jnp.where(valid, result, 0.0)
+        out[n, MAXPNO:] = jnp.zeros((slots - MAXPNO, slots), jnp.float32)
 
 
 def tail(packed, amp, energy):

time: 97 us -> 102 us (1.052)
  Pallas kernels: 96.6 us -> 101 us
    pallas_call x1, Pallas kernels: 94.6 us -> 99.2 us  [pair_products(): pl.pallas_call(main_kernel, out_shape=pltpu.VMEM((PACK, LANES), jnp.float...]
where the time goes in v6:
time: 102 us; the launch traced here: 101 us
  Pallas kernels  101 us (99%)
    pallas_call x1, Pallas kernels, pair_products(): pl.pallas_call(main_kernel, out_shape=pltpu.VMEM((PACK, LANES), jnp.float...  99.2 us

profile of v6, /device:TPU:1, one launch (start us, length us, event | category | flops | bytes accessed | tf_op | source)
XLA Modules:
  0.0 101.5 jit_solution(15721155442903870073)
XLA Ops:
  0.0 0.0 copy-start.1
  0.0 0.0 copy-start
  0.0 99.2 %shard_map.64.packed = f32[640,128]{1,0:T(8,128)S(1)} custom-call(bf16[20,16,1792]{2,1,0:T(8,128)(2,1)} %bitcast.4, s32[12,32]{1,0:T(8,128)} %bitcast.5, s32[32]{0:T(128)} %counts.1, bf16[32,240,256]{2,1,0:T(8,128)(2,1)} %coeff_hbm.1), custom_call_target="tpu_custom_call" | custom-call | tf_op jit(solution)/shard_map/pallas_call | solution.py:927
  99.2 0.0 copy-done.1
  99.2 0.2 copy.7.energy_col
  99.5 0.0 copy-done
  99.5 2.0 %shard_map.65 = f32[4,256,256]{2,1,0:T(8,128)} custom-call(f32[640,128]{1,0:T(8,128)S(1)} %shard_map.64.packed, bf16[4,256,256]{2,1,0:T(8,128)(2,1)S(1)} %copy-done, f32[4,256]{1,0:T(4,128)S(1)} %copy-done.1, f32[4,256,1]{2,1,0:T(8,128)S(1)} %copy.7.energy_col), custom_call_target="tpu_custom_call" | custom-call | tf_op jit(solution)/shard_map/pallas_call | solution.py:1007
Async XLA Ops:
  0.0 99.2 %copy-start.1 = (f32[4,256]{1,0:T(4,128)S(1)}, f32[4,256]{1,0:T(4,128)}, u32[]{:S(2)}) copy-start(f32[4,256]{1,0:T(4,128)} %energy_row.1) | copy-start | bytes 12292
  0.0 99.5 %copy-start = (bf16[4,256,256]{2,1,0:T(8,128)(2,1)S(1)}, bf16[4,256,256]{2,1,0:T(8,128)(2,1)}, u32[]{:S(2)}) copy-start(bf16[4,256,256]{2,1,0:T(8,128)(2,1)} %amp.1) | copy-start | bytes 1572868

commit v7 on v6

--- a/solution.py
+++ b/solution.py
@@ -577,13 +577,9 @@
         lax.fori_loop(begin, end, turn, 0)
 
     prepare(0, 1)
-    for chunk in (2, 3):
-        ports[chunk].start_gather()
     for chunk in (0, 1):
         ports[chunk].forward_gather()
 
-    for single in singles:
-        single.start_gather()
     prepare(1, 3)
 
     own_ask.wait()
@@ -648,16 +644,19 @@
 
     for chunk in (0, 1):
         ports[chunk].finish_gather()
+        ports[chunk + 2].start_gather()
     for chunk in (0, 1):
         ports[chunk].finish_share()
         pick(chunk)
+    for single in singles:
+        single.start_gather()
+    prepare(3, 5)
+    for chunk in (0, 1):
+        ports[chunk].forward_delivery()
     for chunk in (2, 3):
         ports[chunk].forward_gather()
     for single in singles:
         single.forward_gather()
-    prepare(3, 5)
-    for chunk in (0, 1):
-        ports[chunk].forward_delivery()
     prepare(5, 6)
     for chunk in (2, 3):
         ports[chunk].finish_gather()
@@ -840,7 +839,7 @@
 
     fresh[...] = jnp.zeros_like(fresh)
     squares[...] = jnp.zeros_like(squares)
-    ahead = 3
+    ahead = 4
     table_copy.wait()
     ports[0].finish_delivery()
     ports[1].finish_delivery()

time: 102 us -> 100 us (0.980)
  Pallas kernels: 101 us -> 99.6 us
    pallas_call x1, Pallas kernels: 99.2 us -> 97.7 us  [pair_products(): pl.pallas_call(main_kernel, out_shape=pltpu.VMEM((PACK, LANES), jnp.float...]
where the time goes in v7:
time: 100 us; the launch traced here: 99.9 us
  Pallas kernels  99.6 us (100%)
    pallas_call x1, Pallas kernels, pair_products(): pl.pallas_call(main_kernel, out_shape=pltpu.VMEM((PACK, LANES), jnp.float...  97.7 us

profile of v7, /device:TPU:1, one launch (start us, length us, event | category | flops | bytes accessed | tf_op | source)
XLA Modules:
  0.0 99.9 jit_solution(6885293456411170889)
XLA Ops:
  0.0 0.0 copy-start.1
  0.0 0.0 copy-start
  0.0 97.7 %shard_map.64.packed = f32[640,128]{1,0:T(8,128)S(1)} custom-call(bf16[20,16,1792]{2,1,0:T(8,128)(2,1)} %bitcast.4, s32[12,32]{1,0:T(8,128)} %bitcast.5, s32[32]{0:T(128)} %counts.1, bf16[32,240,256]{2,1,0:T(8,128)(2,1)} %coeff_hbm.1), custom_call_target="tpu_custom_call" | custom-call | tf_op jit(solution)/shard_map/pallas_call | solution.py:926
  97.7 0.0 copy-done.1
  97.7 0.2 copy.7.energy_col
  97.9 0.0 copy-done
  97.9 2.0 %shard_map.65 = f32[4,256,256]{2,1,0:T(8,128)} custom-call(f32[640,128]{1,0:T(8,128)S(1)} %shard_map.64.packed, bf16[4,256,256]{2,1,0:T(8,128)(2,1)S(1)} %copy-done, f32[4,256]{1,0:T(4,128)S(1)} %copy-done.1, f32[4,256,1]{2,1,0:T(8,128)S(1)} %copy.7.energy_col), custom_call_target="tpu_custom_call" | custom-call | tf_op jit(solution)/shard_map/pallas_call | solution.py:1006
Async XLA Ops:
  0.0 97.7 %copy-start.1 = (f32[4,256]{1,0:T(4,128)S(1)}, f32[4,256]{1,0:T(4,128)}, u32[]{:S(2)}) copy-start(f32[4,256]{1,0:T(4,128)} %energy_row.1) | copy-start | bytes 12292
  0.0 97.9 %copy-start = (bf16[4,256,256]{2,1,0:T(8,128)(2,1)S(1)}, bf16[4,256,256]{2,1,0:T(8,128)(2,1)}, u32[]{:S(2)}) copy-start(bf16[4,256,256]{2,1,0:T(8,128)(2,1)} %amp.1) | copy-start | bytes 1572868

commit v8 on v5

--- a/solution.py
+++ b/solution.py
@@ -833,7 +833,7 @@
 
     fresh[...] = jnp.zeros_like(fresh)
     squares[...] = jnp.zeros_like(squares)
-    ahead = 4
+    ahead = 5
     table_copy.wait()
     ports[0].finish_delivery()
     ports[1].finish_delivery()
@@ -972,12 +972,13 @@
     on_diagonal = full_row == full_col
     for n in range(2):
         count = packed[pl.ds(COUNTS + 2 * step + n, 1), :][:, :1].astype(jnp.int32)
+        row, col = full_row[:MAXPNO], full_col[:MAXPNO]
         if n == 0:
             held = jnp.where(full_row >= full_col, square, 0.0)
         else:
             held = jnp.where(full_row < full_col, square, jnp.where(on_diagonal, diagonal, 0.0))
-        products = held + jnp.where(on_diagonal, 0.0, held.T)
-        valid = (full_row < count) & (full_col < count)
+        products = held[:MAXPNO] + jnp.where(row == col, 0.0, held.T[:MAXPNO])
+        valid = (row < count) & (col < count)
         products = jnp.where(valid, products / NAUX, 0.0)
         amps = amp[n]
         contract = (((1,), (1,)), ((), ()))
@@ -988,9 +989,10 @@
         coupled = lax.dot_general(low, amps, contract, preferred_element_type=jnp.float32)
         coupled += lax.dot_general(mid, amps, contract, preferred_element_type=jnp.float32)
         coupled += lax.dot_general(high, amps, contract, preferred_element_type=jnp.float32)
-        energies = energy_col[n] + energy_row[pl.ds(2 * step + n, 1), :]
-        result = products + coupled + energies * amps.astype(jnp.float32)
-        out[n] = jnp.where(valid, result, 0.0)
+        energies = energy_col[n, :MAXPNO] + energy_row[pl.ds(2 * step + n, 1), :]
+        result = products + coupled + energies * amps[:MAXPNO].astype(jnp.float32)
+        out[n, :MAXPNO] = jnp.where(valid, result, 0.0)
+        out[n, MAXPNO:] = jnp.zeros((slots - MAXPNO, slots), jnp.float32)
 
 
 def tail(packed, amp, energy):

time: 97 us -> 96.9 us (level); the launches traced: 96.9 us -> 95.8 us
  Pallas kernels: 96.6 us -> 95.5 us
    pallas_call x1, Pallas kernels: 94.6 us -> 93.5 us  [pair_products(): pl.pallas_call(main_kernel, out_shape=pltpu.VMEM((PACK, LANES), jnp.float...]
where the time goes in v8:
time: 96.9 us; the launch traced here: 95.8 us
  Pallas kernels  95.5 us (99%)
    pallas_call x1, Pallas kernels, pair_products(): pl.pallas_call(main_kernel, out_shape=pltpu.VMEM((PACK, LANES), jnp.float...  93.5 us
    pallas_call x1, Pallas kernels, tail(): pl.pallas_call(tail_kernel, out_shape=jax.ShapeDtypeStruct((subs, slots,...  1.98 us

profile of v8, /device:TPU:1, one launch (start us, length us, event | category | flops | bytes accessed | tf_op | source)
XLA Modules:
  0.0 95.8 jit_solution(9328482561905732968)
XLA Ops:
  0.0 0.0 copy-start.1
  0.0 0.0 copy-start
  0.0 93.5 %shard_map.64.packed = f32[640,128]{1,0:T(8,128)S(1)} custom-call(bf16[20,16,1792]{2,1,0:T(8,128)(2,1)} %bitcast.4, s32[12,32]{1,0:T(8,128)} %bitcast.5, s32[32]{0:T(128)} %counts.1, bf16[32,240,256]{2,1,0:T(8,128)(2,1)} %coeff_hbm.1), custom_call_target="tpu_custom_call" | custom-call | tf_op jit(solution)/shard_map/pallas_call | solution.py:920
  93.6 0.0 copy-done.1
  93.6 0.2 copy.7.energy_col
  93.8 0.0 copy-done
  93.8 2.0 %shard_map.65 = f32[4,256,256]{2,1,0:T(8,128)} custom-call(f32[640,128]{1,0:T(8,128)S(1)} %shard_map.64.packed, bf16[4,256,256]{2,1,0:T(8,128)(2,1)S(1)} %copy-done, f32[4,256]{1,0:T(4,128)S(1)} %copy-done.1, f32[4,256,1]{2,1,0:T(8,128)S(1)} %copy.7.energy_col), custom_call_target="tpu_custom_call" | custom-call | tf_op jit(solution)/shard_map/pallas_call | solution.py:1000
Async XLA Ops:
  0.0 93.6 %copy-start.1 = (f32[4,256]{1,0:T(4,128)S(1)}, f32[4,256]{1,0:T(4,128)}, u32[]{:S(2)}) copy-start(f32[4,256]{1,0:T(4,128)} %energy_row.1) | copy-start | bytes 12292
  0.0 93.8 %copy-start = (bf16[4,256,256]{2,1,0:T(8,128)(2,1)S(1)}, bf16[4,256,256]{2,1,0:T(8,128)(2,1)}, u32[]{:S(2)}) copy-start(bf16[4,256,256]{2,1,0:T(8,128)(2,1)} %amp.1) | copy-start | bytes 1572868

commit v9 on v8

--- a/solution.py
+++ b/solution.py
@@ -819,26 +819,20 @@
             add_half(0, step, 0)
             add_half(1, step, 1)
 
-        @pl.when(item == 2)
-        def _():
-            for n in range(len(peers)):
-                ask(n).wait_send()
-            for port in ports:
-                port.finish_sends()
-            for single in singles:
-                single.finish_served()
-                single.finish_sends()
-
         return 0
 
     fresh[...] = jnp.zeros_like(fresh)
     squares[...] = jnp.zeros_like(squares)
-    ahead = 5
+    ahead = 4
     table_copy.wait()
     ports[0].finish_delivery()
     ports[1].finish_delivery()
     assemble(locate(0)[2], 0, (0, 1))
     lax.fori_loop(0, 2 * ahead, first_half, 0)
+    for n in range(len(peers)):
+        ask(n).wait_send()
+    for chunk in (0, 1):
+        ports[chunk].finish_sends()
     for single in singles:
         single.finish_delivery()
     ports[2].finish_delivery()
@@ -847,6 +841,11 @@
     lax.fori_loop(0, ahead, functools.partial(ring_item, False), 0)
     assemble(locate(ahead)[2], 0, (0, 1, 2, 3))
     lax.fori_loop(ahead, planes, functools.partial(ring_item, True), 0)
+    for chunk in (2, 3):
+        ports[chunk].finish_sends()
+    for single in singles:
+        single.finish_served()
+        single.finish_sends()
     for half in (1, 0):
         for piece in range(2):
             rows = rows_of(half, piece)

time: 96.9 us -> 96.9 us (level); the launches traced: 95.8 us -> 96.8 us
  Pallas kernels: 95.5 us -> 96.5 us
    pallas_call x1, Pallas kernels: 93.5 us -> 94.6 us  [pair_products(): pl.pallas_call(main_kernel, out_shape=pltpu.VMEM((PACK, LANES), jnp.float...]
where the time goes in v9:
time: 96.9 us; the launch traced here: 96.8 us
  Pallas kernels  96.5 us (100%)
    pallas_call x1, Pallas kernels, pair_products(): pl.pallas_call(main_kernel, out_shape=pltpu.VMEM((PACK, LANES), jnp.float...  94.6 us
    pallas_call x1, Pallas kernels, tail(): pl.pallas_call(tail_kernel, out_shape=jax.ShapeDtypeStruct((subs, slots,...  1.98 us

profile of v9, /device:TPU:1, one launch (start us, length us, event | category | flops | bytes accessed | tf_op | source)
XLA Modules:
  0.0 96.8 jit_solution(7426127562115097368)
XLA Ops:
  0.0 0.0 copy-start.1
  0.0 0.0 copy-start
  0.0 94.6 %shard_map.64.packed = f32[640,128]{1,0:T(8,128)S(1)} custom-call(bf16[20,16,1792]{2,1,0:T(8,128)(2,1)} %bitcast.4, s32[12,32]{1,0:T(8,128)} %bitcast.5, s32[32]{0:T(128)} %counts.1, bf16[32,240,256]{2,1,0:T(8,128)(2,1)} %coeff_hbm.1), custom_call_target="tpu_custom_call" | custom-call | tf_op jit(solution)/shard_map/pallas_call | solution.py:919
  94.6 0.0 copy-done.1
  94.6 0.2 copy.7.energy_col
  94.8 0.0 copy-done
  94.8 2.0 %shard_map.65 = f32[4,256,256]{2,1,0:T(8,128)} custom-call(f32[640,128]{1,0:T(8,128)S(1)} %shard_map.64.packed, bf16[4,256,256]{2,1,0:T(8,128)(2,1)S(1)} %copy-done, f32[4,256]{1,0:T(4,128)S(1)} %copy-done.1, f32[4,256,1]{2,1,0:T(8,128)S(1)} %copy.7.energy_col), custom_call_target="tpu_custom_call" | custom-call | tf_op jit(solution)/shard_map/pallas_call | solution.py:999
Async XLA Ops:
  0.0 94.6 %copy-start.1 = (f32[4,256]{1,0:T(4,128)S(1)}, f32[4,256]{1,0:T(4,128)}, u32[]{:S(2)}) copy-start(f32[4,256]{1,0:T(4,128)} %energy_row.1) | copy-start | bytes 12292
  0.0 94.8 %copy-start = (bf16[4,256,256]{2,1,0:T(8,128)(2,1)S(1)}, bf16[4,256,256]{2,1,0:T(8,128)(2,1)}, u32[]{:S(2)}) copy-start(bf16[4,256,256]{2,1,0:T(8,128)(2,1)} %amp.1) | copy-start | bytes 1572868
